TPU v7x, 256 devices: a whole 4x4x8 slice. The times are simulated.
256 devices in a mesh: blk: 8 (over y_hi, x), grp: 32 (over z, y_lo, core).
Axes of the slice: x: 4, y: 4 (y_hi: 2, y_lo: 2; y = y_hi * 2 + y_lo), z: 8, core: 2. Of those that a mesh axis runs over, the one named last changes fastest.
Arguments:
- picture_embedding_matrix: bfloat16 [32768, 1152], P(('blk', 'grp')), may hold values from -0.1875 to 0.1875
- caption_embedding_matrix: bfloat16 [32768, 1152], P(('blk', 'grp')), may hold values from -0.1875 to 0.1875
- score_multiplier: float32 [1], replicated, may hold values from 20 to 80
- sigmoid_offset_array: float32 [1], replicated, may hold values from -5 to -3
Outputs:
- visual_steepness: float32 [32768, 1152], P(('blk', 'grp'))
- grad_text: float32 [32768, 1152], P(('blk', 'grp'))
All inputs are finite; a program needn't handle non-finite values.
Results may differ from a plain program's by a relative error of at most 0.0015.
Values may be sent and summed in bfloat16 or wider, within the bound.
A program may use at most 128 MiB of HBM per device.

v0:
```python
import jax
import jax.numpy as jnp
from jax import lax
from jax.sharding import PartitionSpec as P

WINDOW = 2


def shifted(block, axis, distance):
    devices = range(lax.axis_size(axis))
    route = [((i - distance) % len(devices), i) for i in devices]
    return lax.ppermute(block, axis, route)


def per_device(
    picture_embedding_matrix, caption_embedding_matrix, score_multiplier, sigmoid_offset_array
):
    tok_rows = picture_embedding_matrix.shape[0]
    pairs_per_set = tok_rows * lax.axis_size("grp")
    inverse_warmth = score_multiplier[0]
    additive_shift_bias = sigmoid_offset_array[0]
    local_start = lax.axis_index("grp") * tok_rows
    row_ids = lax.broadcasted_iota(jnp.int32, (tok_rows, pairs_per_set), 0) + local_start
    column_indices = lax.broadcasted_iota(jnp.int32, (tok_rows, pairs_per_set), 1)
    positive_labels = (row_ids == column_indices).astype(jnp.float32)
    visual_steepness = jnp.zeros(picture_embedding_matrix.shape, jnp.float32)
    grad_text = jnp.zeros(caption_embedding_matrix.shape, jnp.float32)
    collected_blocks = caption_embedding_matrix
    for hop_index in range(WINDOW):
        text_piece = caption_embedding_matrix
        if hop_index > 0:
            text_piece = shifted(caption_embedding_matrix, "blk", hop_index)
        collected_blocks = lax.all_gather(text_piece, "grp", axis=0, tiled=True)
        similarity_scores = (
            inverse_warmth
            * jnp.einsum(
                "td,gd->tg",
                picture_embedding_matrix,
                collected_blocks,
                preferred_element_type=jnp.float32,
            )
            + additive_shift_bias
        )
        weights = jax.nn.sigmoid(similarity_scores)
        if hop_index == 0:
            weights = weights - positive_labels
        weighting_entries = weights.astype(jnp.bfloat16)
        visual_steepness = visual_steepness + inverse_warmth * jnp.dot(
            weighting_entries, collected_blocks, preferred_element_type=jnp.float32
        )

        def caption_derivative_share(start, count, weighting_entries=weighting_entries):
            inner_multiply = lax.dot_general(
                weighting_entries,
                picture_embedding_matrix,
                (((0,), (0,)), ((), ())),
                preferred_element_type=jnp.float32,
            )
            return inverse_warmth * inner_multiply

        partial_sum = lax.psum_scatter(
            caption_derivative_share(jnp.int32(0), tok_rows * lax.axis_size("grp")),
            "grp",
            scatter_dimension=0,
            tiled=True,
        )
        if hop_index > 0:
            partial_sum = shifted(partial_sum, "blk", -hop_index)
        grad_text = grad_text + partial_sum
    return (visual_steepness, grad_text)


def solution(mesh):
    return jax.shard_map(
        per_device,
        mesh=mesh,
        in_specs=(P(("blk", "grp"), None), P(("blk", "grp"), None), P(), P()),
        out_specs=(P(("blk", "grp"), None), P(("blk", "grp"), None)),
        check_vma=False,
    )
```

profile of v0, /device:TPU:6, one launch (start us, length us, event | category | flops | bytes accessed | tf_op | source)
XLA Modules:
  0.0 604.8 jit_solution(12769447305758997186)
XLA Ops:
  7.2 0.0 copy-start
  7.2 0.0 all-gather.5.cloned.1.call-start
  7.2 3.2 collective-permute-start
  10.4 6.6 %collective-permute-done = bf16[128,1152]{1,0:T(8,128)(2,1)S(1)} collective-permute-done((bf16[128,1152]{1,0:T(8,128)(2,1)}, bf16[128,1152]{1,0:T(8,128)(2,1)S(1)}, u32[]{:S(2)}, u32[]{:S(2)}) %collective-permute-start) | collective-permute-done | bytes 294944 | tf_op jit(solution)/shard_map/ppermute | solution.py:12
  17.0 0.0 copy-start.1
  17.0 0.7 copy-done.1
  17.7 0.0 all-gather.5.cloned.1.call-update
  17.7 0.0 all-gather.3.cloned.1.call-start
  17.8 0.7 all-gather.3.cloned.1.call-update
  18.5 0.0 reduce-scatter.5.cloned.1.call-start
  19.8 74.7 %all-gather.5.cloned.1.call-done = bf16[4096,1152]{1,0:T(8,128)(2,1)} async-done(((bf16[128,1152]{1,0:T(8,128)(2,1)}), bf16[4096,1152]{1,0:T(8,128)(2,1)}) %all-gather.5.cloned.1.call-update) | async-done | bytes 9437200 | tf_op jit(solution)/shard_map/all_gather | solution.py:33
  94.5 0.0 copy-done
  94.5 6.8 %fusion.9 = bf16[128,4096]{1,0:T(8,128)(2,1)S(1)} fusion(bf16[128,1152]{1,0:T(8,128)(2,1)S(1)} %copy-done, bf16[4096,1152]{1,0:T(8,128)(2,1)} %all-gather.5.cloned.1.call-done, f32[]{:T(128)} %bitcast.20, f32[]{:T(128)} %bitcast.18), kind=kOutput, calls=%fused_computation.13 | convolution fusion | flops 1211105280 | bytes 10780680 | tf_op jit(solution)/shard_map/td,gd->tg/dot_general | solution.py:36
  101.4 8.1 %convolution_multiply_fusion = f32[4096,1152]{1,0:T(8,128)} fusion(bf16[128,4096]{1,0:T(8,128)(2,1)S(1)} %fusion.9, bf16[128,1152]{1,0:T(8,128)(2,1)S(1)} %copy-done, f32[]{:T(128)} %bitcast.17), kind=kOutput, calls=%fused_computation | convolution fusion | flops 1212678144 | bytes 20217860 | tf_op jit(solution)/shard_map/dot_general | solution.py:53
  109.5 0.0 reduce-scatter.5.cloned.1.call-update
  109.5 0.0 reduce-scatter.3.cloned.1.call-start
  109.6 59.8 %all-gather.3.cloned.1.call-done = bf16[4096,1152]{1,0:T(8,128)(2,1)} async-done(((bf16[128,1152]{1,0:T(8,128)(2,1)}), bf16[4096,1152]{1,0:T(8,128)(2,1)}) %all-gather.3.cloned.1.call-update) | async-done | bytes 9437200 | tf_op jit(solution)/shard_map/all_gather | solution.py:33
  169.3 6.9 %fusion.12 = bf16[128,4096]{1,0:T(8,128)(2,1)S(1)} fusion(bf16[128,1152]{1,0:T(8,128)(2,1)S(1)} %copy-done, bf16[4096,1152]{1,0:T(8,128)(2,1)} %all-gather.3.cloned.1.call-done, s32[128]{0:T(128)S(1)} %iota_add_fusion, f32[]{:T(128)} %bitcast.19, f32[]{:T(128)} %bitcast.15), kind=kOutput, calls=%fused_computation.16 | convolution fusion | flops 1212678144 | bytes 10781192 | tf_op jit(solution)/shard_map/td,gd->tg/dot_general | solution.py:36
  176.2 8.2 %convolution_multiply_fusion.1 = f32[4096,1152]{1,0:T(8,128)} fusion(bf16[128,4096]{1,0:T(8,128)(2,1)S(1)} %fusion.12, bf16[128,1152]{1,0:T(8,128)(2,1)S(1)} %copy-done, f32[]{:T(128)} %bitcast.16), kind=kOutput, calls=%fused_computation.1 | convolution fusion | flops 1212678144 | bytes 20217860 | tf_op jit(solution)/shard_map/dot_general | solution.py:53
  184.4 0.0 reduce-scatter.3.cloned.1.call-update
  184.5 5.2 fusion.14
  189.7 190.3 %reduce-scatter.5.cloned.1.call-done = f32[128,1152]{1,0:T(8,128)} async-done(((f32[4096,1152]{1,0:T(8,128)}), f32[128,1152]{1,0:T(8,128)}) %reduce-scatter.5.cloned.1.call-update) | async-done | bytes 589840 | tf_op jit(solution)/shard_map/reduce_scatter | solution.py:61
  380.0 0.1 collective-permute-start.1
  380.1 6.0 fusion.13
  386.2 210.2 %reduce-scatter.3.cloned.1.call-done = f32[128,1152]{1,0:T(8,128)} async-done(((f32[4096,1152]{1,0:T(8,128)}), f32[128,1152]{1,0:T(8,128)}) %reduce-scatter.3.cloned.1.call-update) | async-done | bytes 589840 | tf_op jit(solution)/shard_map/reduce_scatter | solution.py:61
  596.4 0.0 collective-permute-done.1
  596.4 1.9 add.41
  (1 shorter events, 0.0 us)
Async XLA Ops:
  7.2 87.4 %copy-start = (bf16[128,1152]{1,0:T(8,128)(2,1)S(1)}, bf16[128,1152]{1,0:T(8,128)(2,1)}, u32[]{:S(2)}) copy-start(bf16[128,1152]{1,0:T(8,128)(2,1)} %param.4) | copy-start | bytes 884740
  7.2 87.3 %all-gather.5.cloned.1.call-start = ((), (), s32[]{:S(2)}) async-start(), calls=%async_computation.3 | async-start | bytes 9732096 | tf_op jit(solution)/shard_map/all_gather | solution.py:33
  7.2 9.8 %collective-permute-start = (bf16[128,1152]{1,0:T(8,128)(2,1)}, bf16[128,1152]{1,0:T(8,128)(2,1)S(1)}, u32[]{:S(2)}, u32[]{:S(2)}) collective-permute-start(bf16[128,1152]{1,0:T(8,128)(2,1)} %param.5), channel_id=1, source_target_pairs={{224,0},{0,32},{32,64},{64,96},{96,128},{128,160},{160,192},{192,2... | collective-permute-start | bytes 884744 | tf_op jit(solution)/shard_map/ppermute | solution.py:12
  17.0 0.7 copy-start.1
  17.7 151.6 %all-gather.3.cloned.1.call-start = ((), (), s32[]{:S(2)}) async-start(), calls=%async_computation.2 | async-start | bytes 9732096 | tf_op jit(solution)/shard_map/all_gather | solution.py:33
  18.5 361.5 %reduce-scatter.5.cloned.1.call-start = ((), (), s32[]{:S(2)}) async-start(), calls=%async_computation.5 | async-start | bytes 19464192 | tf_op jit(solution)/shard_map/reduce_scatter | solution.py:61
  109.5 486.9 %reduce-scatter.3.cloned.1.call-start = ((), (), s32[]{:S(2)}) async-start(), calls=%async_computation.4 | async-start | bytes 19464192 | tf_op jit(solution)/shard_map/reduce_scatter | solution.py:61
  380.0 216.4 %collective-permute-start.1 = (f32[128,1152]{1,0:T(8,128)}, f32[128,1152]{1,0:T(8,128)S(1)}, u32[]{:S(2)}, u32[]{:S(2)}) collective-permute-start(f32[128,1152]{1,0:T(8,128)} %reduce-scatter.5.cloned.1.call-done), channel_id=1, source_target_pairs={{32,0},{64,32},{96,64},{128,96},{160,128},{192,160},{224,192},{0,2... | collective-permute-start | bytes 1769480 | tf_op jit(solution)/shard_map/ppermute | solution.py:12
Sparse Core Ops, SparseCore 0:
  17.9 76.6 all-gather.4
  96.4 72.9 all-gather.2
  171.9 208.0 reduce-scatter.4
  382.4 213.9 reduce-scatter.2
where the time goes:
time: 608 us; the launch traced here: 605 us
  waiting for transfers between devices  542 us (89%)
  matrix products  41.3 us (7%)
  between operations  15.1 us (2%)
    reduce_scatter x2, waiting for transfers between devices, per_device(): lax.psum_scatter(caption_derivative_share(jnp.int32(0), tok_rows * lax.ax...  401 us
    all_gather x2, waiting for transfers between devices, per_device(): collected_blocks = lax.all_gather(text_piece, 'grp', axis=0, tiled=True)  134 us
    dot_general x2, matrix products, caption_derivative_share(): lax.dot_general(weighting_entries, picture_embedding_matrix, (((0,), (0,)...  16.3 us
    dot_general x2, matrix products, per_device(): jnp.einsum('td,gd->tg', picture_embedding_matrix, collected_blocks, prefe...  13.7 us
  transfers between devices with their start and end apart: 6, of which 5 were waited for; matrix products, arithmetic and copies ran while one was open for 7% of the time, Pallas kernels for 0%

commit v1 on v0

v1 whole, which is shorter than its diff:
```python
import functools

import jax
import jax.numpy as jnp
from jax import lax
from jax.experimental import pallas as pl
from jax.experimental.pallas import tpu as pltpu
from jax.sharding import PartitionSpec as P

MESH = pl.DeviceIdType.MESH
LIFT = 2.0**18
TINY = 1e-37
HALF = 64
ROWS = 128
NT = (((1,), (1,)), ((), ()))
TN = (((0,), (0,)), ((), ()))

Z_RIGHT, Z_LEFT = 0, 8
S_RIGHT, S_LEFT = 16, 24
T_CORE, T_Y, T_X = 32, 36, 38
G_CORE, G_Y, G_X = 40, 42, 44
N_SEM = 45


def code(v):
    w = v * LIFT
    w = w * jnp.abs(w)
    w = w * jnp.abs(w)
    return w.astype(jnp.bfloat16)


def decode(u):
    u = u.astype(jnp.float32)
    r = lax.rsqrt(lax.rsqrt(jnp.maximum(jnp.abs(u), TINY))) * (1.0 / LIFT)
    return jnp.where(u < 0.0, -r, r)


def kernel(
    x_ref, t_ref, scale_ref, bias_ref, vis_ref, txt_ref,
    xb, tb, cb, vp, gp, sl, sr, rl, rr, core_out, core_in, y_out, y_in, x_out, x_in, ss, rs, own,
):
    blk = lax.axis_index("blk")
    grp = lax.axis_index("grp")
    z, y, core = grp // 4, (grp // 2) % 2, grp % 2
    right = (blk, ((z + 1) % 8) * 4 + y * 2 + core)
    left = (blk, ((z + 7) % 8) * 4 + y * 2 + core)
    across = (blk, z * 4 + (1 - y) * 2 + core)
    sibling = (blk, z * 4 + y * 2 + (1 - core))
    flip_down = 1 - (blk % 4 + 3) // 4
    up_blk = (blk + 1) % 8
    flip_up = 1 - (up_blk % 4 + 3) // 4
    down = ((blk + 7) % 8, z * 4 + ((y + flip_down) % 2) * 2 + core)
    up = (up_blk, z * 4 + ((y + flip_up) % 2) * 2 + core)

    own_image = pltpu.make_async_copy(x_ref, xb.at[pl.ds(0, ROWS)], own.at[0])
    own_text = pltpu.make_async_copy(t_ref, tb.at[pl.ds(0, ROWS)], own.at[1])
    own_image.start()
    own_text.start()

    barrier = pltpu.get_barrier_semaphore()
    for other in (right, left, across, sibling, down, up):
        pl.semaphore_signal(barrier, inc=1, device_id=other, device_id_type=MESH)
    pl.semaphore_wait(barrier, 6)

    copies = []

    def send(k, src, dst, device):
        copy = pltpu.make_async_remote_copy(
            src_ref=src, dst_ref=dst, send_sem=ss.at[k], recv_sem=rs.at[k],
            device_id=device, device_id_type=MESH,
        )
        copy.start()
        copies.append(copy)
        return copy

    low, high = pl.ds(0, HALF), pl.ds(HALF, HALF)

    def from_left(i):
        return pl.ds(ROWS * i, HALF)

    def from_right(i):
        return pl.ds(ROWS * i + HALF, HALF)

    def text(h, yy, cc):
        return pl.ds(512 * h + 256 * yy + 128 * cc, 128)

    zr, zl, tc = {}, {}, {}
    zr[1] = send(Z_RIGHT + 1, x_ref.at[low], xb.at[from_left(1)], right)
    zl[1] = send(Z_LEFT + 1, x_ref.at[high], xb.at[from_right(1)], left)
    ty0 = send(T_Y, t_ref, tb.at[text(0, 1, 0)], across)
    tx = send(T_X, t_ref, tb.at[text(1, 0, 0)], up)
    tc[0, 0] = send(T_CORE, t_ref, tb.at[text(0, 0, 1)], sibling)
    zr[2] = send(Z_RIGHT + 2, x_ref.at[high], xb.at[from_left(2)], right)
    zl[2] = send(Z_LEFT + 2, x_ref.at[low], xb.at[from_right(2)], left)

    scale = scale_ref[0]
    bias = bias_ref[0]

    def arrive(i):
        zr[i].wait_recv()
        zl[i].wait_recv()
        if i + 2 <= 7:
            zr[i + 2] = send(Z_RIGHT + i + 2, xb.at[from_left(i)], xb.at[from_left(i + 2)], right)
            zl[i + 2] = send(Z_LEFT + i + 2, xb.at[from_right(i)], xb.at[from_right(i + 2)], left)

    def coefficients(start, rows, h):
        x = xb[start : start + rows, :]

        def tile(n, carry):
            cols = pl.ds(pl.multiple_of(n * 256, 256), 256)
            dots = lax.dot_general(x, tb[cols, :], NT, preferred_element_type=jnp.float32)
            away = jnp.minimum(dots * (-scale) - bias, 87.0)
            c = 1.0 / (1.0 + jnp.exp(away))
            if start == 0 and h == 0:
                row = lax.broadcasted_iota(jnp.int32, c.shape, 0)
                col = lax.broadcasted_iota(jnp.int32, c.shape, 1) + n * 256
                c = jnp.where((row == col) & (row < ROWS), c - 1.0, c)
            cb[start : start + rows, cols] = c.astype(jnp.bfloat16)
            return carry

        lax.fori_loop(2 * h, 2 * h + 2, tile, 0)

    def image_terms(start, rows):
        def tile(n, carry):
            cols = pl.ds(pl.multiple_of(n * 384, 384), 384)
            vp[start : start + rows, cols] = jnp.dot(
                cb[start : start + rows, :], tb[:, cols], preferred_element_type=jnp.float32
            )
            return carry

        lax.fori_loop(0, 3, tile, 0)

    def text_terms(h):
        def tile(m, carry):
            cols = pl.ds(pl.multiple_of(m * 256, 256), 256)
            gp[cols, :] = lax.dot_general(cb[:, cols], xb[...], TN, preferred_element_type=jnp.float32)
            return carry

        lax.fori_loop(2 * h, 2 * h + 2, tile, 0)

    vl, vr = {}, {}

    def pass_on(i):
        to_left = vp[ROWS * i : ROWS * i + HALF, :]
        to_right = vp[ROWS * i + HALF : ROWS * (i + 1), :]
        if i <= 5:
            vl[i + 2].wait_recv()
            to_left = to_left + decode(rl[i + 2])
        sl[i] = code(to_left)
        vl[i] = send(S_LEFT + i, sl.at[i], rl.at[i], left)
        if i <= 5:
            vr[i + 2].wait_recv()
            to_right = to_right + decode(rr[i + 2])
        sr[i] = code(to_right)
        vr[i] = send(S_RIGHT + i, sr.at[i], rr.at[i], right)

    def code_rows(dst, src, src_start, count):
        def some(k, carry):
            at = pl.multiple_of(k * 64, 64)
            dst[pl.ds(at, 64), :] = code(src[pl.ds(src_start + at, 64), :])
            return carry

        lax.fori_loop(0, count // 64, some, 0)

    gc = {}

    def text_to_sibling(h):
        for yy in range(2):
            code_rows(core_out.at[h, yy], gp, 512 * h + 256 * yy + 128, 128)
        gc[h] = send(G_CORE + h, core_out.at[h], core_in.at[h], sibling)

    gy = {}

    def text_across(h):
        gc[h].wait_recv()

        def some(k, carry):
            at = pl.ds(pl.multiple_of(k * 64, 64), 64)
            far = pl.ds(512 * h + 256 + pl.multiple_of(k * 64, 64), 64)
            y_out[h, at, :] = code(gp[far, :] + decode(core_in[h, 1, at, :]))
            return carry

        lax.fori_loop(0, 2, some, 0)
        gy[h] = send(G_Y + h, y_out.at[h], y_in.at[h], across)

    def text_sum(h, at, near):
        return gp[near, :] + decode(core_in[h, 0, at, :]) + decode(y_in[h, at, :])

    arrive(1)
    ty0.wait_recv()
    tc[0, 1] = send(T_CORE + 1, tb.at[text(0, 1, 0)], tb.at[text(0, 1, 1)], sibling)
    tx.wait_recv()
    ty1 = send(T_Y + 1, tb.at[text(1, 0, 0)], tb.at[text(1, 1, 0)], across)
    tc[1, 0] = send(T_CORE + 2, tb.at[text(1, 0, 0)], tb.at[text(1, 0, 1)], sibling)
    arrive(2)
    own_text.wait()
    own_image.wait()
    tc[0, 0].wait_recv()
    tc[0, 1].wait_recv()
    coefficients(0, 256, 0)
    arrive(3)
    coefficients(256, 256, 0)
    arrive(4)
    ty1.wait_recv()
    tc[1, 1] = send(T_CORE + 3, tb.at[text(1, 1, 0)], tb.at[text(1, 1, 1)], sibling)
    tc[1, 0].wait_recv()
    tc[1, 1].wait_recv()
    coefficients(0, 256, 1)
    arrive(5)
    coefficients(256, 256, 1)
    coefficients(512, 256, 0)
    coefficients(512, 256, 1)
    arrive(6)
    coefficients(768, 128, 0)
    coefficients(768, 128, 1)
    image_terms(768, 128)
    pass_on(6)
    image_terms(512, 256)
    arrive(7)
    coefficients(896, 128, 0)
    coefficients(896, 128, 1)
    image_terms(896, 128)
    pass_on(7)
    text_terms(1)
    text_to_sibling(1)
    pass_on(4)
    text_terms(0)
    text_to_sibling(0)
    pass_on(5)
    text_across(1)
    text_across(0)
    image_terms(256, 256)
    pass_on(2)
    gy[1].wait_recv()
    for k in range(2):
        at = pl.ds(64 * k, 64)
        x_out[at, :] = code(text_sum(1, at, pl.ds(512 + 64 * k, 64)))
    gx = send(G_X, x_out, x_in, down)
    pass_on(3)
    image_terms(0, 256)
    gy[0].wait_recv()
    for k in range(2):
        at = pl.ds(64 * k, 64)
        gp[at, :] = text_sum(0, at, at)
    pass_on(1)
    gx.wait_recv()
    for k in range(2):
        at = pl.ds(64 * k, 64)
        txt_ref[at, :] = scale * (gp[at, :] + decode(x_in[at, :]))
    vl[2].wait_recv()
    vr[2].wait_recv()
    vp[low, :] = vp[low, :] + decode(rr[2])
    vp[high, :] = vp[high, :] + decode(rl[2])
    vl[1].wait_recv()
    vr[1].wait_recv()
    vis_ref[low, :] = scale * (vp[low, :] + decode(rl[1]))
    vis_ref[high, :] = scale * (vp[high, :] + decode(rr[1]))
    for copy in copies:
        copy.wait_send()


def per_device(images, texts, scale, bias):
    rows, width = images.shape
    bf16, f32 = jnp.bfloat16, jnp.float32
    out = jax.ShapeDtypeStruct((rows, width), f32)
    vmem = pl.BlockSpec(memory_space=pltpu.VMEM)
    hbm = pl.BlockSpec(memory_space=pltpu.HBM)
    smem = pl.BlockSpec(memory_space=pltpu.SMEM)
    return pl.pallas_call(
        kernel,
        out_shape=(out, out),
        in_specs=[hbm, hbm, smem, smem],
        out_specs=(vmem, vmem),
        scratch_shapes=[
            pltpu.VMEM((1024, width), bf16),
            pltpu.VMEM((1024, width), bf16),
            pltpu.VMEM((1024, 1024), bf16),
            pltpu.VMEM((1024, width), f32),
            pltpu.VMEM((1024, width), f32),
            pltpu.VMEM((8, HALF, width), bf16),
            pltpu.VMEM((8, HALF, width), bf16),
            pltpu.VMEM((8, HALF, width), bf16),
            pltpu.VMEM((8, HALF, width), bf16),
            pltpu.VMEM((2, 2, ROWS, width), bf16),
            pltpu.VMEM((2, 2, ROWS, width), bf16),
            pltpu.VMEM((2, ROWS, width), bf16),
            pltpu.VMEM((2, ROWS, width), bf16),
            pltpu.VMEM((ROWS, width), bf16),
            pltpu.VMEM((ROWS, width), bf16),
            pltpu.SemaphoreType.DMA((N_SEM,)),
            pltpu.SemaphoreType.DMA((N_SEM,)),
            pltpu.SemaphoreType.DMA((2,)),
        ],
        compiler_params=pltpu.CompilerParams(
            collective_id=0, has_side_effects=True, vmem_limit_bytes=48 * 1024 * 1024
        ),
        cost_estimate=pl.CostEstimate(
            flops=6 * 1024 * 1024 * width, bytes_accessed=12 * rows * width, transcendentals=2 * 1024 * 1024
        ),
    )(pltpu.with_memory_space_constraint(images, pltpu.HBM), pltpu.with_memory_space_constraint(texts, pltpu.HBM), scale, bias)


def solution(mesh):
    spec = P(("blk", "grp"), None)
    return jax.shard_map(
        per_device,
        mesh=mesh,
        in_specs=(spec, spec, P(), P()),
        out_specs=(spec, spec),
        check_vma=False,
    )
```

time: 608 us -> 67.5 us (0.11)
  the two profiles are of different devices: /device:TPU:6 before, /device:TPU:8 now
where the time goes in v1:
time: 67.5 us; the launch traced here: 67.4 us
  Pallas kernels  63.8 us (95%)
  between operations  1.93 us (3%)
  local copies, waits for them, and re-layouts  1.63 us (2%)
    pallas_call x1, Pallas kernels, per_device(): pl.pallas_call(kernel, out_shape=(out, out), in_specs=[hbm, hbm, smem, sm...  63.8 us
    unnamed x2, local copies, waits for them, and re-layouts  1.63 us

profile of v1, /device:TPU:8, one launch (start us, length us, event | category | flops | bytes accessed | tf_op | source)
XLA Modules:
  0.0 67.4 jit_solution(14487167266202075132)
XLA Ops:
  1.9 63.8 %shard_map.59 = (f32[128,1152]{1,0:T(8,128)S(1)}, f32[128,1152]{1,0:T(8,128)S(1)}) custom-call(bf16[128,1152]{1,0:T(8,128)(2,1)} %x_ref.1, bf16[128,1152]{1,0:T(8,128)(2,1)} %t_ref.1, f32[1]{0:T(128)S(6)} %copy.8.scale_ref, f32[1]{0:T(128)S(6)} %copy.9.bias_ref), custom_call_target="tpu_custom_call" | custom-call | flops 7247757312 | bytes 1769472 | tf_op jit(solution)/shard_map/pallas_call | solution.py:269
  65.7 0.8 %copy.10 = f32[128,1152]{1,0:T(8,128)} copy(f32[128,1152]{1,0:T(8,128)S(1)} %get-tuple-element.4) | data formatting | bytes 1179648
  66.6 0.8 %copy.11 = f32[128,1152]{1,0:T(8,128)} copy(f32[128,1152]{1,0:T(8,128)S(1)} %get-tuple-element.5) | data formatting | bytes 1179648

commit v2 on v1

--- a/solution.py
+++ b/solution.py
@@ -10,16 +10,18 @@
 MESH = pl.DeviceIdType.MESH
 LIFT = 2.0**18
 TINY = 1e-37
+LOG2E = 1.4426950408889634
 HALF = 64
 ROWS = 128
 NT = (((1,), (1,)), ((), ()))
 TN = (((0,), (0,)), ((), ()))
 
 Z_RIGHT, Z_LEFT = 0, 8
-S_RIGHT, S_LEFT = 16, 24
-T_CORE, T_Y, T_X = 32, 36, 38
-G_CORE, G_Y, G_X = 40, 42, 44
-N_SEM = 45
+S_RIGHT, S_LEFT = 16, 32
+T_CORE, T_Y, T_X = 48, 52, 54
+G_CORE, G_Y, G_X = 55, 59, 63
+N_SEM = 65
+PIECES = 2
 
 
 def code(v):
@@ -90,11 +92,14 @@
     ty0 = send(T_Y, t_ref, tb.at[text(0, 1, 0)], across)
     tx = send(T_X, t_ref, tb.at[text(1, 0, 0)], up)
     tc[0, 0] = send(T_CORE, t_ref, tb.at[text(0, 0, 1)], sibling)
+    zr[1].wait_send()
+    zl[1].wait_send()
     zr[2] = send(Z_RIGHT + 2, x_ref.at[high], xb.at[from_left(2)], right)
     zl[2] = send(Z_LEFT + 2, x_ref.at[low], xb.at[from_right(2)], left)
 
     scale = scale_ref[0]
-    bias = bias_ref[0]
+    slope = scale * (-LOG2E)
+    shift = bias_ref[0] * LOG2E
 
     def arrive(i):
         zr[i].wait_recv()
@@ -107,52 +112,47 @@
         x = xb[start : start + rows, :]
 
         def tile(n, carry):
-            cols = pl.ds(pl.multiple_of(n * 256, 256), 256)
-            dots = lax.dot_general(x, tb[cols, :], NT, preferred_element_type=jnp.float32)
-            away = jnp.minimum(dots * (-scale) - bias, 87.0)
-            c = 1.0 / (1.0 + jnp.exp(away))
+            texts = pl.ds(pl.multiple_of(n * 256, 256), 256)
+            dots = lax.dot_general(tb[texts, :], x, NT, preferred_element_type=jnp.float32)
+            away = 1.0 + jnp.exp2(jnp.minimum(dots * slope - shift, 126.0))
+            c = pl.reciprocal(away, approx=True)
+            c = c * (2.0 - away * c)
             if start == 0 and h == 0:
-                row = lax.broadcasted_iota(jnp.int32, c.shape, 0)
-                col = lax.broadcasted_iota(jnp.int32, c.shape, 1) + n * 256
+                row = lax.broadcasted_iota(jnp.int32, c.shape, 0) + n * 256
+                col = lax.broadcasted_iota(jnp.int32, c.shape, 1)
                 c = jnp.where((row == col) & (row < ROWS), c - 1.0, c)
-            cb[start : start + rows, cols] = c.astype(jnp.bfloat16)
+            cb[texts, start : start + rows] = c.astype(jnp.bfloat16)
             return carry
 
         lax.fori_loop(2 * h, 2 * h + 2, tile, 0)
 
-    def image_terms(start, rows):
-        def tile(n, carry):
-            cols = pl.ds(pl.multiple_of(n * 384, 384), 384)
-            vp[start : start + rows, cols] = jnp.dot(
-                cb[start : start + rows, :], tb[:, cols], preferred_element_type=jnp.float32
-            )
-            return carry
-
-        lax.fori_loop(0, 3, tile, 0)
+    def image_terms(start, rows, first, last):
+        texts = pl.ds(512 * first, 512 * (last - first))
+        term = lax.dot_general(
+            cb[texts, start : start + rows], tb[texts, :], TN, preferred_element_type=jnp.float32
+        )
+        if first > 0:
+            term = vp[start : start + rows, :] + term
+        vp[start : start + rows, :] = term
 
     def text_terms(h):
-        def tile(m, carry):
-            cols = pl.ds(pl.multiple_of(m * 256, 256), 256)
-            gp[cols, :] = lax.dot_general(cb[:, cols], xb[...], TN, preferred_element_type=jnp.float32)
-            return carry
-
-        lax.fori_loop(2 * h, 2 * h + 2, tile, 0)
+        texts = pl.ds(512 * h, 512)
+        gp[texts, :] = jnp.dot(cb[texts, :], xb[...], preferred_element_type=jnp.float32)
 
     vl, vr = {}, {}
 
     def pass_on(i):
-        to_left = vp[ROWS * i : ROWS * i + HALF, :]
-        to_right = vp[ROWS * i + HALF : ROWS * (i + 1), :]
-        if i <= 5:
-            vl[i + 2].wait_recv()
-            to_left = to_left + decode(rl[i + 2])
-        sl[i] = code(to_left)
-        vl[i] = send(S_LEFT + i, sl.at[i], rl.at[i], left)
-        if i <= 5:
-            vr[i + 2].wait_recv()
-            to_right = to_right + decode(rr[i + 2])
-        sr[i] = code(to_right)
-        vr[i] = send(S_RIGHT + i, sr.at[i], rr.at[i], right)
+        for p in range(PIECES):
+            part = pl.ds(p * HALF // PIECES, HALF // PIECES)
+            for way, (sent, out, came, to, k) in enumerate(
+                ((vl, sl, rl, left, S_LEFT), (vr, sr, rr, right, S_RIGHT))
+            ):
+                total = vp[pl.ds(ROWS * i + HALF * way + p * HALF // PIECES, HALF // PIECES), :]
+                if i <= 5:
+                    sent[i + 2, p].wait_recv()
+                    total = total + decode(came[i + 2, part, :])
+                out[i, part, :] = code(total)
+                sent[i, p] = send(k + PIECES * i + p, out.at[i, part], came.at[i, part], to)
 
     def code_rows(dst, src, src_start, count):
         def some(k, carry):
@@ -165,26 +165,26 @@
     gc = {}
 
     def text_to_sibling(h):
-        for yy in range(2):
+        for yy in (1, 0):
             code_rows(core_out.at[h, yy], gp, 512 * h + 256 * yy + 128, 128)
-        gc[h] = send(G_CORE + h, core_out.at[h], core_in.at[h], sibling)
+            gc[h, yy] = send(G_CORE + 2 * h + yy, core_out.at[h, yy], core_in.at[h, yy], sibling)
 
     gy = {}
 
     def text_across(h):
-        gc[h].wait_recv()
-
-        def some(k, carry):
-            at = pl.ds(pl.multiple_of(k * 64, 64), 64)
-            far = pl.ds(512 * h + 256 + pl.multiple_of(k * 64, 64), 64)
-            y_out[h, at, :] = code(gp[far, :] + decode(core_in[h, 1, at, :]))
-            return carry
-
-        lax.fori_loop(0, 2, some, 0)
-        gy[h] = send(G_Y + h, y_out.at[h], y_in.at[h], across)
-
-    def text_sum(h, at, near):
-        return gp[near, :] + decode(core_in[h, 0, at, :]) + decode(y_in[h, at, :])
+        gc[h, 1].wait_recv()
+        for k in range(2):
+            at = pl.ds(64 * k, 64)
+            y_out[h, at, :] = code(gp[pl.ds(512 * h + 256 + 64 * k, 64), :] + decode(core_in[h, 1, at, :]))
+            gy[h, k] = send(G_Y + 2 * h + k, y_out.at[h, at], y_in.at[h, at], across)
+
+    def text_sum(h, k):
+        at = pl.ds(64 * k, 64)
+        if k == 0:
+            gc[h, 0].wait_recv()
+        gy[h, k].wait_recv()
+        near = gp[pl.ds(512 * h + 64 * k, 64), :]
+        return near + decode(core_in[h, 0, at, :]) + decode(y_in[h, at, :])
 
     arrive(1)
     ty0.wait_recv()
@@ -200,63 +200,65 @@
     coefficients(0, 256, 0)
     arrive(3)
     coefficients(256, 256, 0)
+    image_terms(0, 512, 0, 1)
     arrive(4)
     ty1.wait_recv()
     tc[1, 1] = send(T_CORE + 3, tb.at[text(1, 1, 0)], tb.at[text(1, 1, 1)], sibling)
+    coefficients(512, 128, 0)
     tc[1, 0].wait_recv()
     tc[1, 1].wait_recv()
     coefficients(0, 256, 1)
     arrive(5)
     coefficients(256, 256, 1)
-    coefficients(512, 256, 0)
+    coefficients(640, 128, 0)
     coefficients(512, 256, 1)
     arrive(6)
     coefficients(768, 128, 0)
     coefficients(768, 128, 1)
-    image_terms(768, 128)
+    image_terms(768, 128, 0, 2)
     pass_on(6)
-    image_terms(512, 256)
+    image_terms(512, 256, 0, 2)
     arrive(7)
     coefficients(896, 128, 0)
     coefficients(896, 128, 1)
-    image_terms(896, 128)
+    image_terms(896, 128, 0, 2)
     pass_on(7)
     text_terms(1)
     text_to_sibling(1)
     pass_on(4)
+    text_across(1)
     text_terms(0)
     text_to_sibling(0)
     pass_on(5)
-    text_across(1)
     text_across(0)
-    image_terms(256, 256)
+    image_terms(0, 512, 1, 2)
     pass_on(2)
-    gy[1].wait_recv()
+    gx = {}
     for k in range(2):
         at = pl.ds(64 * k, 64)
-        x_out[at, :] = code(text_sum(1, at, pl.ds(512 + 64 * k, 64)))
-    gx = send(G_X, x_out, x_in, down)
+        x_out[at, :] = code(text_sum(1, k))
+        gx[k] = send(G_X + k, x_out.at[at], x_in.at[at], down)
     pass_on(3)
-    image_terms(0, 256)
-    gy[0].wait_recv()
+    pass_on(1)
+    for p in range(PIECES):
+        vl[2, p].wait_recv()
+        vr[2, p].wait_recv()
+    vp[low, :] = vp[low, :] + decode(rr[2])
+    vp[high, :] = vp[high, :] + decode(rl[2])
+    for k in range(2):
+        gp[pl.ds(64 * k, 64), :] = text_sum(0, k)
     for k in range(2):
         at = pl.ds(64 * k, 64)
-        gp[at, :] = text_sum(0, at, at)
-    pass_on(1)
-    gx.wait_recv()
-    for k in range(2):
-        at = pl.ds(64 * k, 64)
+        gx[k].wait_recv()
         txt_ref[at, :] = scale * (gp[at, :] + decode(x_in[at, :]))
-    vl[2].wait_recv()
-    vr[2].wait_recv()
-    vp[low, :] = vp[low, :] + decode(rr[2])
-    vp[high, :] = vp[high, :] + decode(rl[2])
-    vl[1].wait_recv()
-    vr[1].wait_recv()
+    for p in range(PIECES):
+        vl[1, p].wait_recv()
+        vr[1, p].wait_recv()
     vis_ref[low, :] = scale * (vp[low, :] + decode(rl[1]))
     vis_ref[high, :] = scale * (vp[high, :] + decode(rr[1]))
     for copy in copies:
-        copy.wait_send()
+        if copy is not zr[1] and copy is not zl[1]:
+            copy.wait_send()
 
 
 def per_device(images, texts, scale, bias):

time: 67.5 us -> 64.9 us (0.961)
  the two profiles are of different devices: /device:TPU:8 before, /device:TPU:1 now
where the time goes in v2:
time: 64.9 us; the launch traced here: 64.8 us
  Pallas kernels  61.2 us (94%)
  between operations  1.93 us (3%)
  local copies, waits for them, and re-layouts  1.63 us (3%)
    pallas_call x1, Pallas kernels, per_device(): pl.pallas_call(kernel, out_shape=(out, out), in_specs=[hbm, hbm, smem, sm...  61.2 us
    unnamed x2, local copies, waits for them, and re-layouts  1.63 us

profile of v2, /device:TPU:1, one launch (start us, length us, event | category | flops | bytes accessed | tf_op | source)
XLA Modules:
  0.0 64.8 jit_solution(12339984283138365773)
XLA Ops:
  1.9 61.2 %shard_map.59 = (f32[128,1152]{1,0:T(8,128)S(1)}, f32[128,1152]{1,0:T(8,128)S(1)}) custom-call(bf16[128,1152]{1,0:T(8,128)(2,1)} %x_ref.1, bf16[128,1152]{1,0:T(8,128)(2,1)} %t_ref.1, f32[1]{0:T(128)S(6)} %copy.8.scale_ref, f32[1]{0:T(128)S(6)} %copy.9.bias_ref), custom_call_target="tpu_custom_call" | custom-call | flops 7247757312 | bytes 1769472 | tf_op jit(solution)/shard_map/pallas_call | solution.py:271
  63.2 0.8 %copy.10 = f32[128,1152]{1,0:T(8,128)} copy(f32[128,1152]{1,0:T(8,128)S(1)} %get-tuple-element.4) | data formatting | bytes 1179648
  64.0 0.8 %copy.11 = f32[128,1152]{1,0:T(8,128)} copy(f32[128,1152]{1,0:T(8,128)S(1)} %get-tuple-element.5) | data formatting | bytes 1179648

commit v3 on v2

--- a/solution.py
+++ b/solution.py
@@ -16,11 +16,11 @@
 NT = (((1,), (1,)), ((), ()))
 TN = (((0,), (0,)), ((), ()))
 
-Z_RIGHT, Z_LEFT = 0, 8
-S_RIGHT, S_LEFT = 16, 32
-T_CORE, T_Y, T_X = 48, 52, 54
-G_CORE, G_Y, G_X = 55, 59, 63
-N_SEM = 65
+Z_RIGHT, Z_LEFT = 0, 16
+S_RIGHT, S_LEFT = 32, 48
+T_CORE, T_Y, T_X = 64, 69, 71
+G_CORE, G_Y, G_X = 73, 77, 81
+N_SEM = 83
 PIECES = 2
 
 
@@ -77,38 +77,46 @@
 
     low, high = pl.ds(0, HALF), pl.ds(HALF, HALF)
 
-    def from_left(i):
-        return pl.ds(ROWS * i, HALF)
-
-    def from_right(i):
-        return pl.ds(ROWS * i + HALF, HALF)
-
     def text(h, yy, cc):
         return pl.ds(512 * h + 256 * yy + 128 * cc, 128)
 
     zr, zl, tc = {}, {}, {}
-    zr[1] = send(Z_RIGHT + 1, x_ref.at[low], xb.at[from_left(1)], right)
-    zl[1] = send(Z_LEFT + 1, x_ref.at[high], xb.at[from_right(1)], left)
+    step = HALF // PIECES
+
+    def go_round(i, p):
+        at = pl.ds(ROWS * i + step * p, step)
+        there = pl.ds(ROWS * i + HALF + step * p, step)
+        if i <= 2:
+            right_start, left_start = (0, HALF) if i == 1 else (HALF, 0)
+            to_right, to_left = x_ref.at[pl.ds(right_start + step * p, step)], x_ref.at[pl.ds(left_start + step * p, step)]
+        else:
+            to_right = xb.at[pl.ds(ROWS * (i - 2) + step * p, step)]
+            to_left = xb.at[pl.ds(ROWS * (i - 2) + HALF + step * p, step)]
+        zr[i, p] = send(Z_RIGHT + PIECES * i + p, to_right, xb.at[at], right)
+        zl[i, p] = send(Z_LEFT + PIECES * i + p, to_left, xb.at[there], left)
+
+    for p in range(PIECES):
+        go_round(1, p)
     ty0 = send(T_Y, t_ref, tb.at[text(0, 1, 0)], across)
     tx = send(T_X, t_ref, tb.at[text(1, 0, 0)], up)
     tc[0, 0] = send(T_CORE, t_ref, tb.at[text(0, 0, 1)], sibling)
-    zr[1].wait_send()
-    zl[1].wait_send()
-    zr[2] = send(Z_RIGHT + 2, x_ref.at[high], xb.at[from_left(2)], right)
-    zl[2] = send(Z_LEFT + 2, x_ref.at[low], xb.at[from_right(2)], left)
+    for p in range(PIECES):
+        zr[1, p].wait_send()
+        zl[1, p].wait_send()
+        go_round(2, p)
 
     scale = scale_ref[0]
     slope = scale * (-LOG2E)
     shift = bias_ref[0] * LOG2E
 
     def arrive(i):
-        zr[i].wait_recv()
-        zl[i].wait_recv()
-        if i + 2 <= 7:
-            zr[i + 2] = send(Z_RIGHT + i + 2, xb.at[from_left(i)], xb.at[from_left(i + 2)], right)
-            zl[i + 2] = send(Z_LEFT + i + 2, xb.at[from_right(i)], xb.at[from_right(i + 2)], left)
-
-    def coefficients(start, rows, h):
+        for p in range(PIECES):
+            zr[i, p].wait_recv()
+            zl[i, p].wait_recv()
+            if i + 2 <= 7:
+                go_round(i + 2, p)
+
+    def coefficients(start, rows, first, last):
         x = xb[start : start + rows, :]
 
         def tile(n, carry):
@@ -117,26 +125,22 @@
             away = 1.0 + jnp.exp2(jnp.minimum(dots * slope - shift, 126.0))
             c = pl.reciprocal(away, approx=True)
             c = c * (2.0 - away * c)
-            if start == 0 and h == 0:
+            if start == 0 and first == 0:
                 row = lax.broadcasted_iota(jnp.int32, c.shape, 0) + n * 256
                 col = lax.broadcasted_iota(jnp.int32, c.shape, 1)
                 c = jnp.where((row == col) & (row < ROWS), c - 1.0, c)
             cb[texts, start : start + rows] = c.astype(jnp.bfloat16)
             return carry
 
-        lax.fori_loop(2 * h, 2 * h + 2, tile, 0)
-
-    def image_terms(start, rows, first, last):
-        texts = pl.ds(512 * first, 512 * (last - first))
-        term = lax.dot_general(
-            cb[texts, start : start + rows], tb[texts, :], TN, preferred_element_type=jnp.float32
+        lax.fori_loop(first, last, tile, 0)
+
+    def image_terms(start, rows):
+        vp[start : start + rows, :] = lax.dot_general(
+            cb[:, start : start + rows], tb[...], TN, preferred_element_type=jnp.float32
         )
-        if first > 0:
-            term = vp[start : start + rows, :] + term
-        vp[start : start + rows, :] = term
-
-    def text_terms(h):
-        texts = pl.ds(512 * h, 512)
+
+    def text_terms(quarter):
+        texts = pl.ds(256 * quarter, 256)
         gp[texts, :] = jnp.dot(cb[texts, :], xb[...], preferred_element_type=jnp.float32)
 
     vl, vr = {}, {}
@@ -164,10 +168,9 @@
 
     gc = {}
 
-    def text_to_sibling(h):
-        for yy in (1, 0):
-            code_rows(core_out.at[h, yy], gp, 512 * h + 256 * yy + 128, 128)
-            gc[h, yy] = send(G_CORE + 2 * h + yy, core_out.at[h, yy], core_in.at[h, yy], sibling)
+    def text_to_sibling(h, yy):
+        code_rows(core_out.at[h, yy], gp, 512 * h + 256 * yy + 128, 128)
+        gc[h, yy] = send(G_CORE + 2 * h + yy, core_out.at[h, yy], core_in.at[h, yy], sibling)
 
     gy = {}
 
@@ -186,59 +189,69 @@
         near = gp[pl.ds(512 * h + 64 * k, 64), :]
         return near + decode(core_in[h, 0, at, :]) + decode(y_in[h, at, :])
 
+    own_text.wait()
+    own_image.wait()
     arrive(1)
+    tc[0, 0].wait_recv()
+    coefficients(0, 256, 0, 1)
     ty0.wait_recv()
+    far_low, far_high = pl.ds(768, HALF), pl.ds(768 + HALF, HALF)
+    tx1 = send(T_X + 1, tb.at[pl.ds(256 + HALF, HALF)], tb.at[far_high], up)
     tc[0, 1] = send(T_CORE + 1, tb.at[text(0, 1, 0)], tb.at[text(0, 1, 1)], sibling)
     tx.wait_recv()
-    ty1 = send(T_Y + 1, tb.at[text(1, 0, 0)], tb.at[text(1, 1, 0)], across)
+    ty1 = send(T_Y + 1, tb.at[pl.ds(512, HALF)], tb.at[far_low], across)
     tc[1, 0] = send(T_CORE + 2, tb.at[text(1, 0, 0)], tb.at[text(1, 0, 1)], sibling)
     arrive(2)
-    own_text.wait()
-    own_image.wait()
-    tc[0, 0].wait_recv()
     tc[0, 1].wait_recv()
-    coefficients(0, 256, 0)
+    tc[1, 0].wait_recv()
+    coefficients(0, 256, 1, 3)
     arrive(3)
-    coefficients(256, 256, 0)
-    image_terms(0, 512, 0, 1)
+    ty1.wait_recv()
+    tc[1, 1] = send(T_CORE + 3, tb.at[far_low], tb.at[pl.ds(896, HALF)], sibling)
+    tx1.wait_recv()
+    tc[1, 2] = send(T_CORE + 4, tb.at[far_high], tb.at[pl.ds(896 + HALF, HALF)], sibling)
+    coefficients(256, 256, 0, 3)
+    tc[1, 1].wait_recv()
+    tc[1, 2].wait_recv()
     arrive(4)
-    ty1.wait_recv()
-    tc[1, 1] = send(T_CORE + 3, tb.at[text(1, 1, 0)], tb.at[text(1, 1, 1)], sibling)
-    coefficients(512, 128, 0)
-    tc[1, 0].wait_recv()
-    tc[1, 1].wait_recv()
-    coefficients(0, 256, 1)
+    coefficients(256, 256, 3, 4)
+    coefficients(0, 256, 3, 4)
+    image_terms(256, 256)
     arrive(5)
-    coefficients(256, 256, 1)
-    coefficients(640, 128, 0)
-    coefficients(512, 256, 1)
+    coefficients(512, 256, 0, 4)
+    image_terms(512, 256)
     arrive(6)
-    coefficients(768, 128, 0)
-    coefficients(768, 128, 1)
-    image_terms(768, 128, 0, 2)
+    coefficients(768, 128, 0, 4)
+    image_terms(768, 128)
     pass_on(6)
-    image_terms(512, 256, 0, 2)
     arrive(7)
-    coefficients(896, 128, 0)
-    coefficients(896, 128, 1)
-    image_terms(896, 128, 0, 2)
+    coefficients(896, 128, 0, 4)
+    image_terms(896, 128)
     pass_on(7)
-    text_terms(1)
-    text_to_sibling(1)
+    text_terms(3)
+    text_to_sibling(1, 1)
     pass_on(4)
     text_across(1)
-    text_terms(0)
-    text_to_sibling(0)
+    text_terms(2)
+    text_to_sibling(1, 0)
     pass_on(5)
-    text_across(0)
-    image_terms(0, 512, 1, 2)
-    pass_on(2)
+    text_terms(1)
+    text_to_sibling(0, 1)
     gx = {}
-    for k in range(2):
+
+    def text_down(k):
         at = pl.ds(64 * k, 64)
         x_out[at, :] = code(text_sum(1, k))
         gx[k] = send(G_X + k, x_out.at[at], x_in.at[at], down)
+
+    text_down(0)
+    pass_on(2)
+    text_across(0)
+    text_down(1)
+    text_terms(0)
+    text_to_sibling(0, 0)
     pass_on(3)
+    image_terms(0, 256)
     pass_on(1)
     for p in range(PIECES):
         vl[2, p].wait_recv()
@@ -250,14 +263,14 @@
     for k in range(2):
         at = pl.ds(64 * k, 64)
         gx[k].wait_recv()
-        txt_ref[at, :] = scale * (gp[at, :] + decode(x_in[at, :]))
+        txt_ref[at, :] = (gp[at, :] + decode(x_in[at, :]))
     for p in range(PIECES):
         vl[1, p].wait_recv()
         vr[1, p].wait_recv()
-    vis_ref[low, :] = scale * (vp[low, :] + decode(rl[1]))
-    vis_ref[high, :] = scale * (vp[high, :] + decode(rr[1]))
+    vis_ref[low, :] = (vp[low, :] + decode(rl[1]))
+    vis_ref[high, :] = (vp[high, :] + decode(rr[1]))
     for copy in copies:
-        if copy is not zr[1] and copy is not zl[1]:
+        if not any(copy is zr[1, p] or copy is zl[1, p] for p in range(PIECES)):
             copy.wait_send()
 
 
@@ -268,7 +281,7 @@
     vmem = pl.BlockSpec(memory_space=pltpu.VMEM)
     hbm = pl.BlockSpec(memory_space=pltpu.HBM)
     smem = pl.BlockSpec(memory_space=pltpu.SMEM)
-    return pl.pallas_call(
+    visual, textual = pl.pallas_call(
         kernel,
         out_shape=(out, out),
         in_specs=[hbm, hbm, smem, smem],
@@ -300,6 +313,7 @@
             flops=6 * 1024 * 1024 * width, bytes_accessed=12 * rows * width, transcendentals=2 * 1024 * 1024
         ),
     )(pltpu.with_memory_space_constraint(images, pltpu.HBM), pltpu.with_memory_space_constraint(texts, pltpu.HBM), scale, bias)
+    return scale[0] * visual, scale[0] * textual
 
 
 def solution(mesh):

time: 64.9 us -> 63.7 us (0.982)
  the two profiles are of different devices: /device:TPU:1 before, /device:TPU:6 now
where the time goes in v3:
time: 63.7 us; the launch traced here: 62.5 us
  Pallas kernels  59.5 us (93%)
  between operations  1.93 us (3%)
  other arithmetic  1.09 us (2%)
    pallas_call x1, Pallas kernels, per_device(): pl.pallas_call(kernel, out_shape=(out, out), in_specs=[hbm, hbm, smem, sm...  59.5 us

profile of v3, /device:TPU:6, one launch (start us, length us, event | category | flops | bytes accessed | tf_op | source)
XLA Modules:
  0.0 62.5 jit_solution(8379587983554601253)
XLA Ops:
  1.9 59.5 %shard_map.59 = (f32[128,1152]{1,0:T(8,128)S(1)}, f32[128,1152]{1,0:T(8,128)S(1)}) custom-call(bf16[128,1152]{1,0:T(8,128)(2,1)} %x_ref.1, bf16[128,1152]{1,0:T(8,128)(2,1)} %t_ref.1, f32[1]{0:T(128)} %copy.6.scale_ref, f32[1]{0:T(128)S(6)} %copy.7.bias_ref), custom_call_target="tpu_custom_call" | custom-call | flops 7247757312 | bytes 1769472 | tf_op jit(solution)/shard_map/pallas_call | solution.py:284
  61.4 1.1 %broadcast_multiply_fusion = (f32[128,1152]{1,0:T(8,128)}, f32[128,1152]{1,0:T(8,128)}) fusion(f32[128,1152]{1,0:T(8,128)S(1)} %get-tuple-element.5, f32[]{:T(128)} %bitcast.1, f32[128,1152]{1,0:T(8,128)S(1)} %get-tuple-element.4), kind=kLoop, calls=%fused_computation | loop fusion | flops 294912 | bytes 2359300 | tf_op jit(solution)/shard_map/mul | solution.py:316

commit v4 on v3

--- a/solution.py
+++ b/solution.py
@@ -39,7 +39,7 @@
 
 def kernel(
     x_ref, t_ref, scale_ref, bias_ref, vis_ref, txt_ref,
-    xb, tb, cb, vp, gp, sl, sr, rl, rr, core_out, core_in, y_out, y_in, x_out, x_in, ss, rs, own,
+    xb, tb, cb, db, vp, gp, sl, sr, rl, rr, core_out, core_in, y_out, y_in, x_out, x_in, ss, rs, own,
 ):
     blk = lax.axis_index("blk")
     grp = lax.axis_index("grp")
@@ -60,9 +60,9 @@
     own_text.start()
 
     barrier = pltpu.get_barrier_semaphore()
-    for other in (right, left, across, sibling, down, up):
+    for other in (right, left, across, sibling, down):
         pl.semaphore_signal(barrier, inc=1, device_id=other, device_id_type=MESH)
-    pl.semaphore_wait(barrier, 6)
+    pl.semaphore_wait(barrier, 5)
 
     copies = []
 
@@ -117,12 +117,14 @@
                 go_round(i + 2, p)
 
     def coefficients(start, rows, first, last):
-        x = xb[start : start + rows, :]
+        some = pl.ds(256 * first, 256 * (last - first))
+        db[some, 0:rows] = lax.dot_general(
+            tb[some, :], xb[start : start + rows, :], NT, preferred_element_type=jnp.float32
+        )
 
         def tile(n, carry):
             texts = pl.ds(pl.multiple_of(n * 256, 256), 256)
-            dots = lax.dot_general(tb[texts, :], x, NT, preferred_element_type=jnp.float32)
-            away = 1.0 + jnp.exp2(jnp.minimum(dots * slope - shift, 126.0))
+            away = 1.0 + jnp.exp2(jnp.minimum(db[texts, 0:rows] * slope - shift, 126.0))
             c = pl.reciprocal(away, approx=True)
             c = c * (2.0 - away * c)
             if start == 0 and first == 0:
@@ -290,6 +292,7 @@
             pltpu.VMEM((1024, width), bf16),
             pltpu.VMEM((1024, width), bf16),
             pltpu.VMEM((1024, 1024), bf16),
+            pltpu.VMEM((1024, 256), f32),
             pltpu.VMEM((1024, width), f32),
             pltpu.VMEM((1024, width), f32),
             pltpu.VMEM((8, HALF, width), bf16),

time: 63.7 us -> 63.3 us (level); the launches traced: 62.5 us -> 63.2 us
  Pallas kernels: 59.5 us -> 60.2 us
    pallas_call x1, Pallas kernels: 59.5 us -> 60.2 us  [per_device(): pl.pallas_call(kernel, out_shape=(out, out), in_specs=[hbm, hbm, smem, sm...]
where the time goes in v4:
time: 63.3 us; the launch traced here: 63.2 us
  Pallas kernels  60.2 us (95%)
  between operations  1.93 us (3%)
  other arithmetic  1.09 us (2%)
    pallas_call x1, Pallas kernels, per_device(): pl.pallas_call(kernel, out_shape=(out, out), in_specs=[hbm, hbm, smem, sm...  60.2 us

profile of v4, /device:TPU:6, one launch (start us, length us, event | category | flops | bytes accessed | tf_op | source)
XLA Modules:
  0.0 63.2 jit_solution(14506175869809363656)
XLA Ops:
  1.9 60.2 %shard_map.59 = (f32[128,1152]{1,0:T(8,128)S(1)}, f32[128,1152]{1,0:T(8,128)S(1)}) custom-call(bf16[128,1152]{1,0:T(8,128)(2,1)} %x_ref.1, bf16[128,1152]{1,0:T(8,128)(2,1)} %t_ref.1, f32[1]{0:T(128)} %copy.6.scale_ref, f32[1]{0:T(128)S(6)} %copy.7.bias_ref), custom_call_target="tpu_custom_call" | custom-call | flops 7247757312 | bytes 1769472 | tf_op jit(solution)/shard_map/pallas_call | solution.py:286
  62.2 1.1 %broadcast_multiply_fusion = (f32[128,1152]{1,0:T(8,128)}, f32[128,1152]{1,0:T(8,128)}) fusion(f32[128,1152]{1,0:T(8,128)S(1)} %get-tuple-element.5, f32[]{:T(128)} %bitcast.1, f32[128,1152]{1,0:T(8,128)S(1)} %get-tuple-element.4), kind=kLoop, calls=%fused_computation | loop fusion | flops 294912 | bytes 2359300 | tf_op jit(solution)/shard_map/mul | solution.py:319

commit v5 on v4

--- a/solution.py
+++ b/solution.py
@@ -20,7 +20,7 @@
 S_RIGHT, S_LEFT = 32, 48
 T_CORE, T_Y, T_X = 64, 69, 71
 G_CORE, G_Y, G_X = 73, 77, 81
-N_SEM = 83
+N_SEM = 84
 PIECES = 2
 
 
@@ -39,7 +39,7 @@
 
 def kernel(
     x_ref, t_ref, scale_ref, bias_ref, vis_ref, txt_ref,
-    xb, tb, cb, db, vp, gp, sl, sr, rl, rr, core_out, core_in, y_out, y_in, x_out, x_in, ss, rs, own,
+    xb, tb, cb, db, vp, gp, sl, sr, rl, rr, core_in, y_out, y_in, x_out, x_in, ss, rs, own,
 ):
     blk = lax.axis_index("blk")
     grp = lax.axis_index("grp")
@@ -160,42 +160,64 @@
                 out[i, part, :] = code(total)
                 sent[i, p] = send(k + PIECES * i + p, out.at[i, part], came.at[i, part], to)
 
-    def code_rows(dst, src, src_start, count):
-        def some(k, carry):
-            at = pl.multiple_of(k * 64, 64)
-            dst[pl.ds(at, 64), :] = code(src[pl.ds(src_start + at, 64), :])
-            return carry
-
-        lax.fori_loop(0, count // 64, some, 0)
-
     gc = {}
 
     def text_to_sibling(h, yy):
-        code_rows(core_out.at[h, yy], gp, 512 * h + 256 * yy + 128, 128)
-        gc[h, yy] = send(G_CORE + 2 * h + yy, core_out.at[h, yy], core_in.at[h, yy], sibling)
-
-    gy = {}
-
-    def text_across(h):
-        gc[h, 1].wait_recv()
-        for k in range(2):
-            at = pl.ds(64 * k, 64)
-            y_out[h, at, :] = code(gp[pl.ds(512 * h + 256 + 64 * k, 64), :] + decode(core_in[h, 1, at, :]))
-            gy[h, k] = send(G_Y + 2 * h + k, y_out.at[h, at], y_in.at[h, at], across)
-
-    def text_sum(h, k):
+        src = gp.at[pl.ds(512 * h + 256 * yy + 128, 128)]
+        gc[h, yy] = send(G_CORE + 2 * h + yy, src, core_in.at[h, yy], sibling)
+
+    gy, gx = {}, {}
+
+    def near_pair(h, yy, k):
+        at = 64 * k
+        ready(h, yy)
+        return gp[pl.ds(512 * h + 256 * yy + at, 64), :] + core_in[h, yy, pl.ds(at, 64), :]
+
+    waited = set()
+
+    def ready(h, yy):
+        if (h, yy) not in waited:
+            waited.add((h, yy))
+            gc[h, yy].wait_recv()
+
+    def far_lower_out():
+        y_out[1, low, :] = code(near_pair(1, 1, 0))
+        gy[1, 0] = send(G_Y + 2, y_out.at[1, low], y_in.at[1, low], across)
+        y_out[1, high, :] = code(near_pair(1, 1, 1))
+        gx[2] = send(G_X + 2, y_out.at[1, high], y_in.at[1, high], down)
+
+    def near_lower_out(k):
         at = pl.ds(64 * k, 64)
+        total = near_pair(1, 0, k)
         if k == 0:
-            gc[h, 0].wait_recv()
-        gy[h, k].wait_recv()
-        near = gp[pl.ds(512 * h + 64 * k, 64), :]
-        return near + decode(core_in[h, 0, at, :]) + decode(y_in[h, at, :])
+            gy[1, 0].wait_recv()
+            total = total + decode(y_in[1, low, :])
+        x_out[at, :] = code(total)
+        gx[k] = send(G_X + k, x_out.at[at], x_in.at[at], down)
+
+    def far_own_out(k):
+        at = pl.ds(64 * k, 64)
+        total = near_pair(0, 1, k)
+        if k == 1:
+            gx[2].wait_recv()
+            total = total + decode(y_in[1, high, :])
+        y_out[0, at, :] = code(total)
+        gy[0, k] = send(G_Y + k, y_out.at[0, at], y_in.at[0, at], across)
+
+    def near_own_sum(k):
+        at = pl.ds(64 * k, 64)
+        total = near_pair(0, 0, k)
+        gy[0, k].wait_recv()
+        total = total + decode(y_in[0, at, :])
+        gx[k].wait_recv()
+        txt_ref[at, :] = total + decode(x_in[at, :])
 
     own_text.wait()
     own_image.wait()
     arrive(1)
     tc[0, 0].wait_recv()
     coefficients(0, 256, 0, 1)
+    arrive(2)
     ty0.wait_recv()
     far_low, far_high = pl.ds(768, HALF), pl.ds(768 + HALF, HALF)
     tx1 = send(T_X + 1, tb.at[pl.ds(256 + HALF, HALF)], tb.at[far_high], up)
@@ -203,7 +225,6 @@
     tx.wait_recv()
     ty1 = send(T_Y + 1, tb.at[pl.ds(512, HALF)], tb.at[far_low], across)
     tc[1, 0] = send(T_CORE + 2, tb.at[text(1, 0, 0)], tb.at[text(1, 0, 1)], sibling)
-    arrive(2)
     tc[0, 1].wait_recv()
     tc[1, 0].wait_recv()
     coefficients(0, 256, 1, 3)
@@ -221,7 +242,6 @@
     image_terms(256, 256)
     arrive(5)
     coefficients(512, 256, 0, 4)
-    image_terms(512, 256)
     arrive(6)
     coefficients(768, 128, 0, 4)
     image_terms(768, 128)
@@ -230,28 +250,23 @@
     coefficients(896, 128, 0, 4)
     image_terms(896, 128)
     pass_on(7)
+    image_terms(512, 256)
+    pass_on(4)
     text_terms(3)
     text_to_sibling(1, 1)
-    pass_on(4)
-    text_across(1)
     text_terms(2)
     text_to_sibling(1, 0)
     pass_on(5)
+    far_lower_out()
+    near_lower_out(1)
     text_terms(1)
     text_to_sibling(0, 1)
-    gx = {}
-
-    def text_down(k):
-        at = pl.ds(64 * k, 64)
-        x_out[at, :] = code(text_sum(1, k))
-        gx[k] = send(G_X + k, x_out.at[at], x_in.at[at], down)
-
-    text_down(0)
     pass_on(2)
-    text_across(0)
-    text_down(1)
     text_terms(0)
     text_to_sibling(0, 0)
+    far_own_out(0)
+    far_own_out(1)
+    near_lower_out(0)
     pass_on(3)
     image_terms(0, 256)
     pass_on(1)
@@ -261,11 +276,7 @@
     vp[low, :] = vp[low, :] + decode(rr[2])
     vp[high, :] = vp[high, :] + decode(rl[2])
     for k in range(2):
-        gp[pl.ds(64 * k, 64), :] = text_sum(0, k)
-    for k in range(2):
-        at = pl.ds(64 * k, 64)
-        gx[k].wait_recv()
-        txt_ref[at, :] = (gp[at, :] + decode(x_in[at, :]))
+        near_own_sum(k)
     for p in range(PIECES):
         vl[1, p].wait_recv()
         vr[1, p].wait_recv()
@@ -299,8 +310,7 @@
             pltpu.VMEM((8, HALF, width), bf16),
             pltpu.VMEM((8, HALF, width), bf16),
             pltpu.VMEM((8, HALF, width), bf16),
-            pltpu.VMEM((2, 2, ROWS, width), bf16),
-            pltpu.VMEM((2, 2, ROWS, width), bf16),
+            pltpu.VMEM((2, 2, ROWS, width), f32),
             pltpu.VMEM((2, ROWS, width), bf16),
             pltpu.VMEM((2, ROWS, width), bf16),
             pltpu.VMEM((ROWS, width), bf16),

time: 63.3 us -> 64 us (1.011)
  Pallas kernels: 60.2 us -> 60.9 us
where the time goes in v5:
time: 64 us; the launch traced here: 63.9 us
  Pallas kernels  60.9 us (95%)
  between operations  1.93 us (3%)
  other arithmetic  1.09 us (2%)
    pallas_call x1, Pallas kernels, per_device(): pl.pallas_call(kernel, out_shape=(out, out), in_specs=[hbm, hbm, smem, sm...  60.9 us

profile of v5, /device:TPU:6, one launch (start us, length us, event | category | flops | bytes accessed | tf_op | source)
XLA Modules:
  0.0 63.9 jit_solution(3878882612445823781)
XLA Ops:
  1.9 60.9 %shard_map.59 = (f32[128,1152]{1,0:T(8,128)S(1)}, f32[128,1152]{1,0:T(8,128)S(1)}) custom-call(bf16[128,1152]{1,0:T(8,128)(2,1)} %x_ref.1, bf16[128,1152]{1,0:T(8,128)(2,1)} %t_ref.1, f32[1]{0:T(128)} %copy.6.scale_ref, f32[1]{0:T(128)S(6)} %copy.7.bias_ref), custom_call_target="tpu_custom_call" | custom-call | flops 7247757312 | bytes 1769472 | tf_op jit(solution)/shard_map/pallas_call | solution.py:297
  62.8 1.1 %broadcast_multiply_fusion = (f32[128,1152]{1,0:T(8,128)}, f32[128,1152]{1,0:T(8,128)}) fusion(f32[128,1152]{1,0:T(8,128)S(1)} %get-tuple-element.5, f32[]{:T(128)} %bitcast.1, f32[128,1152]{1,0:T(8,128)S(1)} %get-tuple-element.4), kind=kLoop, calls=%fused_computation | loop fusion | flops 294912 | bytes 2359300 | tf_op jit(solution)/shard_map/mul | solution.py:329

commit v6 on v4

--- a/solution.py
+++ b/solution.py
@@ -196,29 +196,30 @@
     arrive(1)
     tc[0, 0].wait_recv()
     coefficients(0, 256, 0, 1)
+    arrive(2)
     ty0.wait_recv()
     far_low, far_high = pl.ds(768, HALF), pl.ds(768 + HALF, HALF)
     tx1 = send(T_X + 1, tb.at[pl.ds(256 + HALF, HALF)], tb.at[far_high], up)
     tc[0, 1] = send(T_CORE + 1, tb.at[text(0, 1, 0)], tb.at[text(0, 1, 1)], sibling)
+    tc[0, 1].wait_recv()
+    coefficients(0, 256, 1, 2)
+    arrive(3)
     tx.wait_recv()
     ty1 = send(T_Y + 1, tb.at[pl.ds(512, HALF)], tb.at[far_low], across)
     tc[1, 0] = send(T_CORE + 2, tb.at[text(1, 0, 0)], tb.at[text(1, 0, 1)], sibling)
-    arrive(2)
-    tc[0, 1].wait_recv()
+    coefficients(256, 256, 0, 2)
     tc[1, 0].wait_recv()
-    coefficients(0, 256, 1, 3)
-    arrive(3)
+    coefficients(0, 256, 2, 3)
+    coefficients(256, 256, 2, 3)
+    arrive(4)
     ty1.wait_recv()
     tc[1, 1] = send(T_CORE + 3, tb.at[far_low], tb.at[pl.ds(896, HALF)], sibling)
     tx1.wait_recv()
     tc[1, 2] = send(T_CORE + 4, tb.at[far_high], tb.at[pl.ds(896 + HALF, HALF)], sibling)
-    coefficients(256, 256, 0, 3)
     tc[1, 1].wait_recv()
     tc[1, 2].wait_recv()
-    arrive(4)
+    coefficients(0, 256, 3, 4)
     coefficients(256, 256, 3, 4)
-    coefficients(0, 256, 3, 4)
-    image_terms(256, 256)
     arrive(5)
     coefficients(512, 256, 0, 4)
     image_terms(512, 256)
@@ -239,6 +240,8 @@
     pass_on(5)
     text_terms(1)
     text_to_sibling(0, 1)
+    image_terms(256, 256)
+    pass_on(2)
     gx = {}
 
     def text_down(k):
@@ -247,12 +250,11 @@
         gx[k] = send(G_X + k, x_out.at[at], x_in.at[at], down)
 
     text_down(0)
-    pass_on(2)
     text_across(0)
-    text_down(1)
     text_terms(0)
     text_to_sibling(0, 0)
     pass_on(3)
+    text_down(1)
     image_terms(0, 256)
     pass_on(1)
     for p in range(PIECES):

time: 63.3 us -> 62.6 us (0.989)
  Pallas kernels: 60.2 us -> 59.2 us
    pallas_call x1, Pallas kernels: 60.2 us -> 59.2 us  [per_device(): pl.pallas_call(kernel, out_shape=(out, out), in_specs=[hbm, hbm, smem, sm...]
where the time goes in v6:
time: 62.6 us; the launch traced here: 62.2 us
  Pallas kernels  59.2 us (95%)
  between operations  1.93 us (3%)
  other arithmetic  1.09 us (2%)
    pallas_call x1, Pallas kernels, per_device(): pl.pallas_call(kernel, out_shape=(out, out), in_specs=[hbm, hbm, smem, sm...  59.2 us

profile of v6, /device:TPU:6, one launch (start us, length us, event | category | flops | bytes accessed | tf_op | source)
XLA Modules:
  0.0 62.2 jit_solution(5379724037390870910)
XLA Ops:
  1.9 59.2 %shard_map.59 = (f32[128,1152]{1,0:T(8,128)S(1)}, f32[128,1152]{1,0:T(8,128)S(1)}) custom-call(bf16[128,1152]{1,0:T(8,128)(2,1)} %x_ref.1, bf16[128,1152]{1,0:T(8,128)(2,1)} %t_ref.1, f32[1]{0:T(128)} %copy.6.scale_ref, f32[1]{0:T(128)S(6)} %copy.7.bias_ref), custom_call_target="tpu_custom_call" | custom-call | flops 7247757312 | bytes 1769472 | tf_op jit(solution)/shard_map/pallas_call | solution.py:288
  61.1 1.1 %broadcast_multiply_fusion = (f32[128,1152]{1,0:T(8,128)}, f32[128,1152]{1,0:T(8,128)}) fusion(f32[128,1152]{1,0:T(8,128)S(1)} %get-tuple-element.5, f32[]{:T(128)} %bitcast.1, f32[128,1152]{1,0:T(8,128)S(1)} %get-tuple-element.4), kind=kLoop, calls=%fused_computation | loop fusion | flops 294912 | bytes 2359300 | tf_op jit(solution)/shard_map/mul | solution.py:321

commit v7 on v6

--- a/solution.py
+++ b/solution.py
@@ -201,16 +201,14 @@
     far_low, far_high = pl.ds(768, HALF), pl.ds(768 + HALF, HALF)
     tx1 = send(T_X + 1, tb.at[pl.ds(256 + HALF, HALF)], tb.at[far_high], up)
     tc[0, 1] = send(T_CORE + 1, tb.at[text(0, 1, 0)], tb.at[text(0, 1, 1)], sibling)
-    tc[0, 1].wait_recv()
-    coefficients(0, 256, 1, 2)
-    arrive(3)
     tx.wait_recv()
     ty1 = send(T_Y + 1, tb.at[pl.ds(512, HALF)], tb.at[far_low], across)
     tc[1, 0] = send(T_CORE + 2, tb.at[text(1, 0, 0)], tb.at[text(1, 0, 1)], sibling)
-    coefficients(256, 256, 0, 2)
+    tc[0, 1].wait_recv()
     tc[1, 0].wait_recv()
-    coefficients(0, 256, 2, 3)
-    coefficients(256, 256, 2, 3)
+    coefficients(0, 256, 1, 3)
+    arrive(3)
+    coefficients(256, 256, 0, 3)
     arrive(4)
     ty1.wait_recv()
     tc[1, 1] = send(T_CORE + 3, tb.at[far_low], tb.at[pl.ds(896, HALF)], sibling)

time: 62.6 us -> 62.6 us (level)
  no operation moved by 1% of the time
where the time goes in v7:
time: 62.6 us; the launch traced here: 61.9 us
  Pallas kernels  58.9 us (94%)
  between operations  1.93 us (3%)
  other arithmetic  1.09 us (2%)
    pallas_call x1, Pallas kernels, per_device(): pl.pallas_call(kernel, out_shape=(out, out), in_specs=[hbm, hbm, smem, sm...  58.9 us

profile of v7, /device:TPU:6, one launch (start us, length us, event | category | flops | bytes accessed | tf_op | source)
XLA Modules:
  0.0 61.9 jit_solution(8179244071222344549)
XLA Ops:
  1.9 58.9 %shard_map.59 = (f32[128,1152]{1,0:T(8,128)S(1)}, f32[128,1152]{1,0:T(8,128)S(1)}) custom-call(bf16[128,1152]{1,0:T(8,128)(2,1)} %x_ref.1, bf16[128,1152]{1,0:T(8,128)(2,1)} %t_ref.1, f32[1]{0:T(128)} %copy.6.scale_ref, f32[1]{0:T(128)S(6)} %copy.7.bias_ref), custom_call_target="tpu_custom_call" | custom-call | flops 7247757312 | bytes 1769472 | tf_op jit(solution)/shard_map/pallas_call | solution.py:286
  60.8 1.1 %broadcast_multiply_fusion = (f32[128,1152]{1,0:T(8,128)}, f32[128,1152]{1,0:T(8,128)}) fusion(f32[128,1152]{1,0:T(8,128)S(1)} %get-tuple-element.5, f32[]{:T(128)} %bitcast.1, f32[128,1152]{1,0:T(8,128)S(1)} %get-tuple-element.4), kind=kLoop, calls=%fused_computation | loop fusion | flops 294912 | bytes 2359300 | tf_op jit(solution)/shard_map/mul | solution.py:319

commit v8 on v7

--- a/solution.py
+++ b/solution.py
@@ -136,10 +136,14 @@
 
         lax.fori_loop(first, last, tile, 0)
 
-    def image_terms(start, rows):
-        vp[start : start + rows, :] = lax.dot_general(
-            cb[:, start : start + rows], tb[...], TN, preferred_element_type=jnp.float32
+    def image_terms(start, rows, first, last):
+        texts = pl.ds(256 * first, 256 * (last - first))
+        term = lax.dot_general(
+            cb[texts, start : start + rows], tb[texts, :], TN, preferred_element_type=jnp.float32
         )
+        if first > 0:
+            term = vp[start : start + rows, :] + term
+        vp[start : start + rows, :] = term
 
     def text_terms(quarter):
         texts = pl.ds(256 * quarter, 256)
@@ -209,6 +213,7 @@
     coefficients(0, 256, 1, 3)
     arrive(3)
     coefficients(256, 256, 0, 3)
+    image_terms(0, 512, 0, 2)
     arrive(4)
     ty1.wait_recv()
     tc[1, 1] = send(T_CORE + 3, tb.at[far_low], tb.at[pl.ds(896, HALF)], sibling)
@@ -218,16 +223,17 @@
     tc[1, 2].wait_recv()
     coefficients(0, 256, 3, 4)
     coefficients(256, 256, 3, 4)
+    image_terms(256, 256, 2, 4)
     arrive(5)
     coefficients(512, 256, 0, 4)
-    image_terms(512, 256)
+    image_terms(512, 256, 0, 4)
     arrive(6)
     coefficients(768, 128, 0, 4)
-    image_terms(768, 128)
+    image_terms(768, 128, 0, 4)
     pass_on(6)
     arrive(7)
     coefficients(896, 128, 0, 4)
-    image_terms(896, 128)
+    image_terms(896, 128, 0, 4)
     pass_on(7)
     text_terms(3)
     text_to_sibling(1, 1)
@@ -238,7 +244,6 @@
     pass_on(5)
     text_terms(1)
     text_to_sibling(0, 1)
-    image_terms(256, 256)
     pass_on(2)
     gx = {}
 
@@ -253,7 +258,7 @@
     text_to_sibling(0, 0)
     pass_on(3)
     text_down(1)
-    image_terms(0, 256)
+    image_terms(0, 256, 2, 4)
     pass_on(1)
     for p in range(PIECES):
         vl[2, p].wait_recv()

time: 62.6 us -> 63 us (level)
  no operation moved by 1% of the time
where the time goes in v8:
time: 63 us; the launch traced here: 62.5 us
  Pallas kernels  59.4 us (94%)
  between operations  1.93 us (3%)
  other arithmetic  1.09 us (2%)
    pallas_call x1, Pallas kernels, per_device(): pl.pallas_call(kernel, out_shape=(out, out), in_specs=[hbm, hbm, smem, sm...  59.4 us

profile of v8, /device:TPU:6, one launch (start us, length us, event | category | flops | bytes accessed | tf_op | source)
XLA Modules:
  0.0 62.5 jit_solution(3778032373482547836)
XLA Ops:
  1.9 59.4 %shard_map.59 = (f32[128,1152]{1,0:T(8,128)S(1)}, f32[128,1152]{1,0:T(8,128)S(1)}) custom-call(bf16[128,1152]{1,0:T(8,128)(2,1)} %x_ref.1, bf16[128,1152]{1,0:T(8,128)(2,1)} %t_ref.1, f32[1]{0:T(128)} %copy.6.scale_ref, f32[1]{0:T(128)S(6)} %copy.7.bias_ref), custom_call_target="tpu_custom_call" | custom-call | flops 7247757312 | bytes 1769472 | tf_op jit(solution)/shard_map/pallas_call | solution.py:291
  61.4 1.1 %broadcast_multiply_fusion = (f32[128,1152]{1,0:T(8,128)}, f32[128,1152]{1,0:T(8,128)}) fusion(f32[128,1152]{1,0:T(8,128)S(1)} %get-tuple-element.5, f32[]{:T(128)} %bitcast.1, f32[128,1152]{1,0:T(8,128)S(1)} %get-tuple-element.4), kind=kLoop, calls=%fused_computation | loop fusion | flops 294912 | bytes 2359300 | tf_op jit(solution)/shard_map/mul | solution.py:324

commit v9 on v8

--- a/solution.py
+++ b/solution.py
@@ -54,14 +54,13 @@
     down = ((blk + 7) % 8, z * 4 + ((y + flip_down) % 2) * 2 + core)
     up = (up_blk, z * 4 + ((y + flip_up) % 2) * 2 + core)
 
+    barrier = pltpu.get_barrier_semaphore()
+    for other in (right, left, across, sibling, down):
+        pl.semaphore_signal(barrier, inc=1, device_id=other, device_id_type=MESH)
     own_image = pltpu.make_async_copy(x_ref, xb.at[pl.ds(0, ROWS)], own.at[0])
     own_text = pltpu.make_async_copy(t_ref, tb.at[pl.ds(0, ROWS)], own.at[1])
     own_image.start()
     own_text.start()
-
-    barrier = pltpu.get_barrier_semaphore()
-    for other in (right, left, across, sibling, down):
-        pl.semaphore_signal(barrier, inc=1, device_id=other, device_id_type=MESH)
     pl.semaphore_wait(barrier, 5)
 
     copies = []
@@ -145,14 +144,15 @@
             term = vp[start : start + rows, :] + term
         vp[start : start + rows, :] = term
 
-    def text_terms(quarter):
+    def text_terms(quarter, part):
         texts = pl.ds(256 * quarter, 256)
-        gp[texts, :] = jnp.dot(cb[texts, :], xb[...], preferred_element_type=jnp.float32)
+        cols = (pl.ds(0, 640), pl.ds(640, 512))[part]
+        gp[texts, cols] = jnp.dot(cb[texts, :], xb[:, cols], preferred_element_type=jnp.float32)
 
     vl, vr = {}, {}
 
-    def pass_on(i):
-        for p in range(PIECES):
+    def pass_on(i, pieces=range(PIECES)):
+        for p in pieces:
             part = pl.ds(p * HALF // PIECES, HALF // PIECES)
             for way, (sent, out, came, to, k) in enumerate(
                 ((vl, sl, rl, left, S_LEFT), (vr, sr, rr, right, S_RIGHT))
@@ -235,16 +235,6 @@
     coefficients(896, 128, 0, 4)
     image_terms(896, 128, 0, 4)
     pass_on(7)
-    text_terms(3)
-    text_to_sibling(1, 1)
-    pass_on(4)
-    text_across(1)
-    text_terms(2)
-    text_to_sibling(1, 0)
-    pass_on(5)
-    text_terms(1)
-    text_to_sibling(0, 1)
-    pass_on(2)
     gx = {}
 
     def text_down(k):
@@ -252,11 +242,29 @@
         x_out[at, :] = code(text_sum(1, k))
         gx[k] = send(G_X + k, x_out.at[at], x_in.at[at], down)
 
+    text_terms(3, 0)
+    pass_on(4, [0])
+    text_terms(3, 1)
+    text_to_sibling(1, 1)
+    pass_on(4, [1])
+    text_terms(2, 0)
+    text_across(1)
+    pass_on(5, [0])
+    text_terms(2, 1)
+    text_to_sibling(1, 0)
+    pass_on(5, [1])
+    text_terms(1, 0)
+    pass_on(2, [0])
+    text_terms(1, 1)
+    text_to_sibling(0, 1)
+    pass_on(2, [1])
     text_down(0)
+    text_terms(0, 0)
     text_across(0)
-    text_terms(0)
+    pass_on(3, [0])
+    text_terms(0, 1)
     text_to_sibling(0, 0)
-    pass_on(3)
+    pass_on(3, [1])
     text_down(1)
     image_terms(0, 256, 2, 4)
     pass_on(1)

time: 63 us -> 63 us (level)
  no operation moved by 1% of the time
where the time goes in v9:
time: 63 us; the launch traced here: 62.5 us
  Pallas kernels  59.4 us (94%)
  between operations  1.93 us (3%)
  other arithmetic  1.09 us (2%)
    pallas_call x1, Pallas kernels, per_device(): pl.pallas_call(kernel, out_shape=(out, out), in_specs=[hbm, hbm, smem, sm...  59.4 us

profile of v9, /device:TPU:6, one launch (start us, length us, event | category | flops | bytes accessed | tf_op | source)
XLA Modules:
  0.0 62.5 jit_solution(15670412817408697653)
XLA Ops:
  1.9 59.4 %shard_map.59 = (f32[128,1152]{1,0:T(8,128)S(1)}, f32[128,1152]{1,0:T(8,128)S(1)}) custom-call(bf16[128,1152]{1,0:T(8,128)(2,1)} %x_ref.1, bf16[128,1152]{1,0:T(8,128)(2,1)} %t_ref.1, f32[1]{0:T(128)} %copy.6.scale_ref, f32[1]{0:T(128)S(6)} %copy.7.bias_ref), custom_call_target="tpu_custom_call" | custom-call | flops 7247757312 | bytes 1769472 | tf_op jit(solution)/shard_map/pallas_call | solution.py:299
  61.4 1.1 %broadcast_multiply_fusion = (f32[128,1152]{1,0:T(8,128)}, f32[128,1152]{1,0:T(8,128)}) fusion(f32[128,1152]{1,0:T(8,128)S(1)} %get-tuple-element.5, f32[]{:T(128)} %bitcast.1, f32[128,1152]{1,0:T(8,128)S(1)} %get-tuple-element.4), kind=kLoop, calls=%fused_computation | loop fusion | flops 294912 | bytes 2359300 | tf_op jit(solution)/shard_map/mul | solution.py:332

commit v10 on v8

--- a/solution.py
+++ b/solution.py
@@ -16,12 +16,14 @@
 NT = (((1,), (1,)), ((), ()))
 TN = (((0,), (0,)), ((), ()))
 
-Z_RIGHT, Z_LEFT = 0, 16
-S_RIGHT, S_LEFT = 32, 48
-T_CORE, T_Y, T_X = 64, 69, 71
-G_CORE, G_Y, G_X = 73, 77, 81
-N_SEM = 83
-PIECES = 2
+PIECES = 4
+Z_RIGHT, Z_LEFT = 0, 8 * PIECES
+S_RIGHT, S_LEFT = 16 * PIECES, 24 * PIECES
+T_CORE = 32 * PIECES
+T_Y, T_X = T_CORE + 5, T_CORE + 7
+G_CORE = T_CORE + 9
+G_Y, G_X = G_CORE + 4, G_CORE + 8
+N_SEM = G_CORE + 10
 
 
 def code(v):
@@ -54,14 +56,13 @@
     down = ((blk + 7) % 8, z * 4 + ((y + flip_down) % 2) * 2 + core)
     up = (up_blk, z * 4 + ((y + flip_up) % 2) * 2 + core)
 
+    barrier = pltpu.get_barrier_semaphore()
+    for other in (right, left, across, sibling, down):
+        pl.semaphore_signal(barrier, inc=1, device_id=other, device_id_type=MESH)
     own_image = pltpu.make_async_copy(x_ref, xb.at[pl.ds(0, ROWS)], own.at[0])
     own_text = pltpu.make_async_copy(t_ref, tb.at[pl.ds(0, ROWS)], own.at[1])
     own_image.start()
     own_text.start()
-
-    barrier = pltpu.get_barrier_semaphore()
-    for other in (right, left, across, sibling, down):
-        pl.semaphore_signal(barrier, inc=1, device_id=other, device_id_type=MESH)
     pl.semaphore_wait(barrier, 5)
 
     copies = []

time: 63 us -> 63.3 us (level)
  Pallas kernels: 59.4 us -> 60.2 us
    pallas_call x1, Pallas kernels: 59.4 us -> 60.2 us  [per_device(): pl.pallas_call(kernel, out_shape=(out, out), in_specs=[hbm, hbm, smem, sm...]
where the time goes in v10:
time: 63.3 us; the launch traced here: 63.2 us
  Pallas kernels  60.2 us (95%)
  between operations  1.93 us (3%)
  other arithmetic  1.09 us (2%)
    pallas_call x1, Pallas kernels, per_device(): pl.pallas_call(kernel, out_shape=(out, out), in_specs=[hbm, hbm, smem, sm...  60.2 us

profile of v10, /device:TPU:6, one launch (start us, length us, event | category | flops | bytes accessed | tf_op | source)
XLA Modules:
  0.0 63.2 jit_solution(7999734492101878632)
XLA Ops:
  1.9 60.2 %shard_map.59 = (f32[128,1152]{1,0:T(8,128)S(1)}, f32[128,1152]{1,0:T(8,128)S(1)}) custom-call(bf16[128,1152]{1,0:T(8,128)(2,1)} %x_ref.1, bf16[128,1152]{1,0:T(8,128)(2,1)} %t_ref.1, f32[1]{0:T(128)} %copy.6.scale_ref, f32[1]{0:T(128)S(6)} %copy.7.bias_ref), custom_call_target="tpu_custom_call" | custom-call | flops 7247757312 | bytes 1769472 | tf_op jit(solution)/shard_map/pallas_call | solution.py:292
  62.1 1.1 %broadcast_multiply_fusion = (f32[128,1152]{1,0:T(8,128)}, f32[128,1152]{1,0:T(8,128)}) fusion(f32[128,1152]{1,0:T(8,128)S(1)} %get-tuple-element.5, f32[]{:T(128)} %bitcast.1, f32[128,1152]{1,0:T(8,128)S(1)} %get-tuple-element.4), kind=kLoop, calls=%fused_computation | loop fusion | flops 294912 | bytes 2359300 | tf_op jit(solution)/shard_map/mul | solution.py:325

commit v11 on v8

--- a/solution.py
+++ b/solution.py
@@ -54,14 +54,13 @@
     down = ((blk + 7) % 8, z * 4 + ((y + flip_down) % 2) * 2 + core)
     up = (up_blk, z * 4 + ((y + flip_up) % 2) * 2 + core)
 
+    barrier = pltpu.get_barrier_semaphore()
+    for other in (right, left, across, sibling, down):
+        pl.semaphore_signal(barrier, inc=1, device_id=other, device_id_type=MESH)
     own_image = pltpu.make_async_copy(x_ref, xb.at[pl.ds(0, ROWS)], own.at[0])
     own_text = pltpu.make_async_copy(t_ref, tb.at[pl.ds(0, ROWS)], own.at[1])
     own_image.start()
     own_text.start()
-
-    barrier = pltpu.get_barrier_semaphore()
-    for other in (right, left, across, sibling, down):
-        pl.semaphore_signal(barrier, inc=1, device_id=other, device_id_type=MESH)
     pl.semaphore_wait(barrier, 5)
 
     copies = []
@@ -151,15 +150,20 @@
 
     vl, vr = {}, {}
 
+    def pieces(i):
+        return 2 if i in (1, 3) else 1
+
     def pass_on(i):
-        for p in range(PIECES):
-            part = pl.ds(p * HALF // PIECES, HALF // PIECES)
+        rows = HALF // pieces(i)
+        for p in range(pieces(i)):
+            part = pl.ds(p * rows, rows)
             for way, (sent, out, came, to, k) in enumerate(
                 ((vl, sl, rl, left, S_LEFT), (vr, sr, rr, right, S_RIGHT))
             ):
-                total = vp[pl.ds(ROWS * i + HALF * way + p * HALF // PIECES, HALF // PIECES), :]
+                total = vp[pl.ds(ROWS * i + HALF * way + p * rows, rows), :]
                 if i <= 5:
-                    sent[i + 2, p].wait_recv()
+                    if p < pieces(i + 2):
+                        sent[i + 2, p].wait_recv()
                     total = total + decode(came[i + 2, part, :])
                 out[i, part, :] = code(total)
                 sent[i, p] = send(k + PIECES * i + p, out.at[i, part], came.at[i, part], to)
@@ -260,9 +264,8 @@
     text_down(1)
     image_terms(0, 256, 2, 4)
     pass_on(1)
-    for p in range(PIECES):
-        vl[2, p].wait_recv()
-        vr[2, p].wait_recv()
+    vl[2, 0].wait_recv()
+    vr[2, 0].wait_recv()
     vp[low, :] = vp[low, :] + decode(rr[2])
     vp[high, :] = vp[high, :] + decode(rl[2])
     for k in range(2):
@@ -270,12 +273,13 @@
     for k in range(2):
         at = pl.ds(64 * k, 64)
         gx[k].wait_recv()
-        txt_ref[at, :] = (gp[at, :] + decode(x_in[at, :]))
-    for p in range(PIECES):
+        txt_ref[at, :] = gp[at, :] + decode(x_in[at, :])
+    for p in range(2):
+        part, upper = pl.ds(32 * p, 32), pl.ds(HALF + 32 * p, 32)
         vl[1, p].wait_recv()
+        vis_ref[part, :] = vp[part, :] + decode(rl[1, part, :])
         vr[1, p].wait_recv()
-    vis_ref[low, :] = (vp[low, :] + decode(rl[1]))
-    vis_ref[high, :] = (vp[high, :] + decode(rr[1]))
+        vis_ref[upper, :] = vp[upper, :] + decode(rr[1, part, :])
     for copy in copies:
         if not any(copy is zr[1, p] or copy is zl[1, p] for p in range(PIECES)):
             copy.wait_send()

time: 63 us -> 62.4 us (level)
  no operation moved by 1% of the time
where the time goes in v11:
time: 62.4 us; the launch traced here: 62.3 us
  Pallas kernels  59.3 us (95%)
  between operations  1.93 us (3%)
  other arithmetic  1.09 us (2%)
    pallas_call x1, Pallas kernels, per_device(): pl.pallas_call(kernel, out_shape=(out, out), in_specs=[hbm, hbm, smem, sm...  59.3 us

profile of v11, /device:TPU:6, one launch (start us, length us, event | category | flops | bytes accessed | tf_op | source)
XLA Modules:
  0.0 62.3 jit_solution(12293807727080783847)
XLA Ops:
  1.9 59.3 %shard_map.59 = (f32[128,1152]{1,0:T(8,128)S(1)}, f32[128,1152]{1,0:T(8,128)S(1)}) custom-call(bf16[128,1152]{1,0:T(8,128)(2,1)} %x_ref.1, bf16[128,1152]{1,0:T(8,128)(2,1)} %t_ref.1, f32[1]{0:T(128)} %copy.6.scale_ref, f32[1]{0:T(128)S(6)} %copy.7.bias_ref), custom_call_target="tpu_custom_call" | custom-call | flops 7247757312 | bytes 1769472 | tf_op jit(solution)/shard_map/pallas_call | solution.py:295
  61.2 1.1 %broadcast_multiply_fusion = (f32[128,1152]{1,0:T(8,128)}, f32[128,1152]{1,0:T(8,128)}) fusion(f32[128,1152]{1,0:T(8,128)S(1)} %get-tuple-element.5, f32[]{:T(128)} %bitcast.1, f32[128,1152]{1,0:T(8,128)S(1)} %get-tuple-element.4), kind=kLoop, calls=%fused_computation | loop fusion | flops 294912 | bytes 2359300 | tf_op jit(solution)/shard_map/mul | solution.py:328

commit v12 on v11

--- a/solution.py
+++ b/solution.py
@@ -260,8 +260,8 @@
     text_across(0)
     text_terms(0)
     text_to_sibling(0, 0)
+    text_down(1)
     pass_on(3)
-    text_down(1)
     image_terms(0, 256, 2, 4)
     pass_on(1)
     vl[2, 0].wait_recv()

time: 62.4 us -> 62.4 us (level)
  no operation moved by 1% of the time
where the time goes in v12:
time: 62.4 us; the launch traced here: 62.3 us
  Pallas kernels  59.3 us (95%)
  between operations  1.93 us (3%)
  other arithmetic  1.09 us (2%)
    pallas_call x1, Pallas kernels, per_device(): pl.pallas_call(kernel, out_shape=(out, out), in_specs=[hbm, hbm, smem, sm...  59.3 us

profile of v12, /device:TPU:6, one launch (start us, length us, event | category | flops | bytes accessed | tf_op | source)
XLA Modules:
  0.0 62.3 jit_solution(8643041656554302894)
XLA Ops:
  1.9 59.3 %shard_map.59 = (f32[128,1152]{1,0:T(8,128)S(1)}, f32[128,1152]{1,0:T(8,128)S(1)}) custom-call(bf16[128,1152]{1,0:T(8,128)(2,1)} %x_ref.1, bf16[128,1152]{1,0:T(8,128)(2,1)} %t_ref.1, f32[1]{0:T(128)} %copy.6.scale_ref, f32[1]{0:T(128)S(6)} %copy.7.bias_ref), custom_call_target="tpu_custom_call" | custom-call | flops 7247757312 | bytes 1769472 | tf_op jit(solution)/shard_map/pallas_call | solution.py:295
  61.2 1.1 %broadcast_multiply_fusion = (f32[128,1152]{1,0:T(8,128)}, f32[128,1152]{1,0:T(8,128)}) fusion(f32[128,1152]{1,0:T(8,128)S(1)} %get-tuple-element.5, f32[]{:T(128)} %bitcast.1, f32[128,1152]{1,0:T(8,128)S(1)} %get-tuple-element.4), kind=kLoop, calls=%fused_computation | loop fusion | flops 294912 | bytes 2359300 | tf_op jit(solution)/shard_map/mul | solution.py:328

commit v13 on v11

--- a/solution.py
+++ b/solution.py
@@ -100,8 +100,6 @@
     tx = send(T_X, t_ref, tb.at[text(1, 0, 0)], up)
     tc[0, 0] = send(T_CORE, t_ref, tb.at[text(0, 0, 1)], sibling)
     for p in range(PIECES):
-        zr[1, p].wait_send()
-        zl[1, p].wait_send()
         go_round(2, p)
 
     scale = scale_ref[0]
@@ -281,8 +279,7 @@
         vr[1, p].wait_recv()
         vis_ref[upper, :] = vp[upper, :] + decode(rr[1, part, :])
     for copy in copies:
-        if not any(copy is zr[1, p] or copy is zl[1, p] for p in range(PIECES)):
-            copy.wait_send()
+        copy.wait_send()
 
 
 def per_device(images, texts, scale, bias):

time: 62.4 us -> 62.5 us (level)
  no operation moved by 1% of the time
where the time goes in v13:
time: 62.5 us; the launch traced here: 62.3 us
  Pallas kernels  59.3 us (95%)
  between operations  1.93 us (3%)
  other arithmetic  1.09 us (2%)
    pallas_call x1, Pallas kernels, per_device(): pl.pallas_call(kernel, out_shape=(out, out), in_specs=[hbm, hbm, smem, sm...  59.3 us

profile of v13, /device:TPU:6, one launch (start us, length us, event | category | flops | bytes accessed | tf_op | source)
XLA Modules:
  0.0 62.3 jit_solution(14145253605029411950)
XLA Ops:
  1.9 59.3 %shard_map.59 = (f32[128,1152]{1,0:T(8,128)S(1)}, f32[128,1152]{1,0:T(8,128)S(1)}) custom-call(bf16[128,1152]{1,0:T(8,128)(2,1)} %x_ref.1, bf16[128,1152]{1,0:T(8,128)(2,1)} %t_ref.1, f32[1]{0:T(128)} %copy.6.scale_ref, f32[1]{0:T(128)S(6)} %copy.7.bias_ref), custom_call_target="tpu_custom_call" | custom-call | flops 7247757312 | bytes 1769472 | tf_op jit(solution)/shard_map/pallas_call | solution.py:292
  61.2 1.1 %broadcast_multiply_fusion = (f32[128,1152]{1,0:T(8,128)}, f32[128,1152]{1,0:T(8,128)}) fusion(f32[128,1152]{1,0:T(8,128)S(1)} %get-tuple-element.5, f32[]{:T(128)} %bitcast.1, f32[128,1152]{1,0:T(8,128)S(1)} %get-tuple-element.4), kind=kLoop, calls=%fused_computation | loop fusion | flops 294912 | bytes 2359300 | tf_op jit(solution)/shard_map/mul | solution.py:325

commit v14 on v13

--- a/solution.py
+++ b/solution.py
@@ -204,11 +204,9 @@
     coefficients(0, 256, 0, 1)
     arrive(2)
     ty0.wait_recv()
-    far_low, far_high = pl.ds(768, HALF), pl.ds(768 + HALF, HALF)
-    tx1 = send(T_X + 1, tb.at[pl.ds(256 + HALF, HALF)], tb.at[far_high], up)
     tc[0, 1] = send(T_CORE + 1, tb.at[text(0, 1, 0)], tb.at[text(0, 1, 1)], sibling)
     tx.wait_recv()
-    ty1 = send(T_Y + 1, tb.at[pl.ds(512, HALF)], tb.at[far_low], across)
+    ty1 = send(T_Y + 1, tb.at[text(1, 0, 0)], tb.at[text(1, 1, 0)], across)
     tc[1, 0] = send(T_CORE + 2, tb.at[text(1, 0, 0)], tb.at[text(1, 0, 1)], sibling)
     tc[0, 1].wait_recv()
     tc[1, 0].wait_recv()
@@ -218,11 +216,8 @@
     image_terms(0, 512, 0, 2)
     arrive(4)
     ty1.wait_recv()
-    tc[1, 1] = send(T_CORE + 3, tb.at[far_low], tb.at[pl.ds(896, HALF)], sibling)
-    tx1.wait_recv()
-    tc[1, 2] = send(T_CORE + 4, tb.at[far_high], tb.at[pl.ds(896 + HALF, HALF)], sibling)
+    tc[1, 1] = send(T_CORE + 3, tb.at[text(1, 1, 0)], tb.at[text(1, 1, 1)], sibling)
     tc[1, 1].wait_recv()
-    tc[1, 2].wait_recv()
     coefficients(0, 256, 3, 4)
     coefficients(256, 256, 3, 4)
     image_terms(256, 256, 2, 4)

time: 62.5 us -> 63.4 us (1.014); the launches traced: 62.3 us -> 62.3 us
  no operation moved by 1% of the time
where the time goes in v14:
time: 63.4 us; the launch traced here: 62.3 us
  Pallas kernels  59.3 us (94%)
  between operations  1.93 us (3%)
  other arithmetic  1.09 us (2%)
    pallas_call x1, Pallas kernels, per_device(): pl.pallas_call(kernel, out_shape=(out, out), in_specs=[hbm, hbm, smem, sm...  59.3 us

profile of v14, /device:TPU:6, one launch (start us, length us, event | category | flops | bytes accessed | tf_op | source)
XLA Modules:
  0.0 62.3 jit_solution(17808363326829377754)
XLA Ops:
  1.9 59.3 %shard_map.59 = (f32[128,1152]{1,0:T(8,128)S(1)}, f32[128,1152]{1,0:T(8,128)S(1)}) custom-call(bf16[128,1152]{1,0:T(8,128)(2,1)} %x_ref.1, bf16[128,1152]{1,0:T(8,128)(2,1)} %t_ref.1, f32[1]{0:T(128)} %copy.6.scale_ref, f32[1]{0:T(128)S(6)} %copy.7.bias_ref), custom_call_target="tpu_custom_call" | custom-call | flops 7247757312 | bytes 1769472 | tf_op jit(solution)/shard_map/pallas_call | solution.py:287
  61.2 1.1 %broadcast_multiply_fusion = (f32[128,1152]{1,0:T(8,128)}, f32[128,1152]{1,0:T(8,128)}) fusion(f32[128,1152]{1,0:T(8,128)S(1)} %get-tuple-element.5, f32[]{:T(128)} %bitcast.1, f32[128,1152]{1,0:T(8,128)S(1)} %get-tuple-element.4), kind=kLoop, calls=%fused_computation | loop fusion | flops 294912 | bytes 2359300 | tf_op jit(solution)/shard_map/mul | solution.py:320
